TPU v7x, 32 devices: a whole 2x2x4 slice. The times are simulated.
32 devices in a mesh: groups: 2 (over y), seq: 16 (over z, x, core).
Axes of the slice: x: 2, y: 2, z: 4, core: 2. Of those that a mesh axis runs over, the one named last changes fastest.
Arguments:
- frames: bfloat16 [64, 32, 128, 128], P(('groups', 'seq')), parts along dimension 0, may hold values from -6 to 6
- w_spatial: bfloat16 [3, 3, 128, 128], replicated, may hold values from -0.1875 to 0.1875
- w_temporal: bfloat16 [2, 3, 128, 128], replicated, may hold values from -0.3125 to 0.3125
- dilations: int32 [2], replicated, may hold values from 1 to 16
- offsets: int32 [2, 3], replicated, may hold values from 0 to 3
- cotangent: bfloat16 [64, 1024, 128], P('groups', 'seq'), parts along dimension 0, may hold values from -0.011962891 to 0.011962891
Outputs:
- features: bfloat16 [64, 1024, 128], P('groups', 'seq'), parts along dimension 0
- grad_spatial: float32 [6, 3, 128, 128], P('groups'), parts along dimension 0
- grad_temporal: float32 [4, 3, 128, 128], P('groups'), parts along dimension 0
There are 2 independent parts, one for each index of `groups`. A program takes and returns all parts, laid end to end along the dimension named above; an argument that names none is the same for every part. Nothing has to cross between parts.
All inputs are finite; a program needn't handle non-finite values.
Results may differ from a plain program's by a relative error of at most 0.0067.
Values may be sent and summed in bfloat16 or wider, within the bound.
A program may use at most 64 MiB of HBM per device.

v0:
```python
import jax
import jax.numpy as jnp
from jax import lax
from jax.sharding import PartitionSpec as P


def padded_view(frames):
    count, height, width, channels = frames.shape
    padded = jnp.pad(frames, ((0, 0), (1, 1), (1, 1), (0, 0)))
    return padded.reshape(count, height // 2 + 1, 2, width // 2 + 1, 2, channels)


def window(view, row_tap, col_tap):
    out_rows = view.shape[1] - 1
    out_cols = view.shape[3] - 1
    return view[
        :,
        row_tap // 2 : row_tap // 2 + out_rows,
        row_tap % 2,
        col_tap // 2 : col_tap // 2 + out_cols,
        col_tap % 2,
        :,
    ]


def delayed(values, delay):
    length = values.shape[0]
    delay = jnp.minimum(delay, length)
    joined = jnp.concatenate([jnp.zeros_like(values), values], 0)
    return lax.dynamic_slice_in_dim(joined, length - delay, length, 0)


def advanced(values, delay):
    length = values.shape[0]
    delay = jnp.minimum(delay, length)
    joined = jnp.concatenate([values, jnp.zeros_like(values)], 0)
    return lax.dynamic_slice_in_dim(joined, delay, length, 0)


def temporal_forward(start, w_temporal, delays):
    length, pixels, channels = start.shape
    states = [start]
    activations = []
    for layer in range(w_temporal.shape[0]):
        state = states[-1]
        total = jnp.zeros((length * pixels, channels), jnp.float32)
        for tap in range(w_temporal.shape[1]):
            moved = delayed(state, delays[layer, tap]).reshape(-1, channels)
            total = total + jnp.dot(
                moved, w_temporal[layer, tap], preferred_element_type=jnp.float32
            )
        activ = jnp.tanh(total).reshape(length, pixels, channels)
        activations.append(activ)
        states.append((state.astype(jnp.float32) + activ).astype(jnp.bfloat16))
    return (states, activations)


def temporal_backward(states, activations, cotangent, w_temporal, delays):
    length, pixels, channels = cotangent.shape
    layer_count = w_temporal.shape[0]
    grad_state = cotangent.astype(jnp.float32)
    grads = [None] * layer_count
    for layer in reversed(range(layer_count)):
        activ = activations[layer]
        dz_flat = (grad_state * (1.0 - activ * activ)).astype(jnp.bfloat16).reshape(-1, channels)
        layer_grads = []
        for tap in range(w_temporal.shape[1]):
            moved = delayed(states[layer], delays[layer, tap]).reshape(-1, channels)
            layer_grads.append(
                lax.dot_general(
                    moved, dz_flat, (((0,), (0,)), ((), ())), preferred_element_type=jnp.float32
                )
            )
            backward = jnp.dot(
                dz_flat, w_temporal[layer, tap].T, preferred_element_type=jnp.float32
            )
            grad_state = grad_state + advanced(
                backward.reshape(length, pixels, channels), delays[layer, tap]
            )
        grads[layer] = jnp.stack(layer_grads)
    return (grad_state.astype(jnp.bfloat16), jnp.stack(grads))


def local(frames, w_spatial, w_temporal, dilations, offsets, cotangent):
    count, height, width, channels = frames.shape
    map_pixels = height // 2 * (width // 2)
    delays = offsets * dilations[:, None]
    view = padded_view(frames)
    total = jnp.zeros((count * map_pixels, channels), jnp.float32)
    for row_tap in range(3):
        for col_tap in range(3):
            patch = window(view, row_tap, col_tap).reshape(-1, channels)
            total = total + jnp.dot(
                patch, w_spatial[row_tap, col_tap], preferred_element_type=jnp.float32
            )
    spatial = total.astype(jnp.bfloat16).reshape(count, map_pixels, channels)
    gathered = lax.all_to_all(spatial, "seq", split_axis=1, concat_axis=0, tiled=True)
    states, activations = temporal_forward(gathered, w_temporal, delays)
    grad_maps, local_temporal = temporal_backward(
        states, activations, cotangent, w_temporal, delays
    )
    back = lax.all_to_all(grad_maps, "seq", split_axis=0, concat_axis=1, tiled=True)
    back_flat = back.reshape(-1, channels)
    rows = []
    for row_tap in range(3):
        cols = []
        for col_tap in range(3):
            patch = window(view, row_tap, col_tap).reshape(-1, channels)
            cols.append(
                lax.dot_general(
                    patch, back_flat, (((0,), (0,)), ((), ())), preferred_element_type=jnp.float32
                )
            )
        rows.append(jnp.stack(cols))
    local_spatial = jnp.stack(rows)
    grad_spatial, grad_temporal = lax.psum((local_spatial, local_temporal), "seq")
    return (states[-1], grad_spatial, grad_temporal)


def solution(mesh):
    in_specs = (
        P(("groups", "seq"), None, None, None),
        P(),
        P(),
        P(),
        P(),
        P("groups", "seq", None),
    )
    out_specs = (
        P("groups", "seq", None),
        P("groups", None, None, None),
        P("groups", None, None, None),
    )
    return jax.shard_map(local, mesh=mesh, in_specs=in_specs, out_specs=out_specs, check_vma=False)
```

profile of v0, /device:TPU:1, one launch (start us, length us, event | category | flops | bytes accessed | tf_op | source)
XLA Modules:
  0.0 180.6 jit_solution(3432139852399982071)
XLA Ops:
  7.2 3.8 %copy.37 = bf16[2,32,128,128]{3,0,2,1:T(2,128)(2,1)S(1)} copy(bf16[2,32,128,128]{3,2,1,0:T(8,128)(2,1)} %param.6) | data formatting | bytes 4194304
  10.9 1.7 pad.12.clone
  12.7 3.9 %fusion.62 = (bf16[2,16,1,64,1,128]{5,0,4,3,2,1:T(2,128)(2,1)S(1)}, bf16[2,16,1,64,1,128]{5,0,4,3,2,1:T(2,128)(2,1)S(1)}, bf16[2,16,1,64,1,128]{5,0,4,3,2,1:T(2,...) fusion(bf16[2,17,2,65,2,128]{5,0,4,3,2,1:T(2,128)(2,1)S(1)} %bi, ...), kind=kLoop, calls=%fused_computation.113 | loop fusion | bytes 9437184 | tf_op jit(solution)/shard_map/slice | solution.py:16
  17.8 0.7 copy-done.14
  19.3 0.3 convolution_add_fusion.9
  19.9 0.3 convolution_add_fusion.7
  20.5 0.3 convolution_add_fusion.5
  21.1 1.3 copy.34
  22.4 7.4 %all-to-all-start = ((bf16[2,1024,128]{2,0,1:T(2,128)(2,1)}), bf16[2,1024,128]{2,0,1:T(2,128)(2,1)S(1)}, u32[]{:S(2)}, u32[]{:S(2)}) async-start(bf16[2,1024,128]{2,0,1:T(2,128)(2,1)} %copy.34), calls=%async_computation | async-start | bytes 1048576 | tf_op jit(solution)/shard_map/all_to_all | solution.py:97
  29.9 0.7 fusion.63
  34.5 9.4 %all-to-all-done = bf16[2,1024,128]{2,0,1:T(2,128)(2,1)S(1)} async-done(((bf16[2,1024,128]{2,0,1:T(2,128)(2,1)}), bf16[2,1024,128]{2,0,1:T(2,128)(2,1)S(1)}, u32[]{:S(2)}, u32[]{:S(2)}) %all-to-all-start) | async-done | bytes 524320 | tf_op jit(solution)/shard_map/all_to_all | solution.py:97
  44.0 0.8 pad_dynamic-slice_fusion.9
  45.8 0.3 fusion.1
  46.3 0.8 pad_dynamic-slice_fusion.6
  47.7 0.3 fusion
  48.0 0.5 copy-done.12
  48.4 1.1 fusion.3
  49.5 0.3 convolution_bitcast_fusion
  49.9 0.3 convolution_bitcast_fusion.1
  50.2 0.3 convolution_bitcast_fusion.2
  50.6 0.3 fusion.16
  50.9 0.3 fusion.18
  51.2 0.3 fusion.20
  51.5 0.7 multiply_convert_fusion
  52.2 0.3 fusion.10
  52.5 0.3 fusion.12
  52.8 0.3 fusion.14
  53.0 1.4 fusion.9
  54.4 4.5 %all-to-all-start.1 = ((bf16[32,64,128]{2,1,0:T(8,128)(2,1)}), bf16[32,64,128]{2,1,0:T(8,128)(2,1)}, u32[]{:S(2)}, u32[]{:S(2)}) async-start(bf16[32,64,128]{2,1,0:T(8,128)(2,1)} %fusion.9), calls=%async_computation.1 | async-start | bytes 1048576 | tf_op jit(solution)/shard_map/all_to_all | solution.py:102
  59.0 1.4 convolution_bitcast_fusion.3
  60.4 1.4 convolution_bitcast_fusion.4
  61.8 0.3 convolution_bitcast_fusion.5
  62.1 0.8 pad_maximum_fusion.1
  62.9 10.2 %all-to-all-done.1 = bf16[32,64,128]{2,1,0:T(8,128)(2,1)} async-done(((bf16[32,64,128]{2,1,0:T(8,128)(2,1)}), bf16[32,64,128]{2,1,0:T(8,128)(2,1)}, u32[]{:S(2)}, u32[]{:S(2)}) %all-to-all-start.1) | async-done | bytes 524320 | tf_op jit(solution)/shard_map/all_to_all | solution.py:102
  73.2 1.1 copy.36
  74.3 0.3 convolution_bitcast_fusion.6
  74.7 0.4 convolution_bitcast_fusion.7
  75.0 0.4 convolution_bitcast_fusion.8
  75.4 0.3 convolution_bitcast_fusion.9
  75.8 0.3 convolution_bitcast_fusion.10
  76.1 0.3 convolution_bitcast_fusion.11
  76.5 0.3 convolution_bitcast_fusion.12
  76.8 0.3 convolution_bitcast_fusion.13
  77.2 0.3 convolution_bitcast_fusion.14
  77.6 0.9 pad_maximum_fusion
  78.5 91.6 %all-reduce.12.cloned.1.call-done = (f32[3,3,128,128]{3,2,1,0:T(8,128)}, f32[2,3,128,128]{3,2,1,0:T(8,128)}) async-done(((f32[3,3,128,128]{3,2,1,0:T(8,128)}, f32[2,3,128,128]{3,2,1,0:T(8,128)}), (f32[3,3,128,128]{3,2,1,0:T(8,128)}, f32[2,3,128,128]{3,2,1,0:T(8,128)})) %all-reduce.12.cloned.1.call-update) | async-done | bytes 983056 | tf_op jit(solution)/shard_map/psum | solution.py:116
  170.1 1.9 %copy.40 = f32[3,3,128,128]{3,2,1,0:T(8,128)} copy(f32[3,3,128,128]{3,2,1,0:T(8,128)} %get-tuple-element.33) | data formatting | bytes 1179648
  172.0 1.8 copy.41
  (60 shorter events, 4.7 us)
Async XLA Ops:
  17.1 2.8 %copy-start = (bf16[2,16,1,64,1,128]{5,3,1,0,4,2:T(8,128)(2,1)}, bf16[2,16,1,64,1,128]{5,3,1,0,4,2:T(8,128)(2,1)S(1)}, u32[]{:S(2)}) copy-start(bf16[2,16,1,64,1,128]{5,3,1,0,4,2:T(8,128)(2,1)S(1)} %copy.30) | copy-start | bytes 1572868
  17.2 2.4 %copy-start.2 = (bf16[2,16,1,64,1,128]{5,3,1,0,4,2:T(8,128)(2,1)}, bf16[2,16,1,64,1,128]{5,3,1,0,4,2:T(8,128)(2,1)S(1)}, u32[]{:S(2)}) copy-start(bf16[2,16,1,64,1,128]{5,3,1,0,4,2:T(8,128)(2,1)S(1)} %copy.29) | copy-start | bytes 1572868
  17.2 1.2 copy-start.14
  17.4 1.9 %copy-start.4 = (bf16[2,16,1,64,1,128]{5,3,1,0,4,2:T(8,128)(2,1)}, bf16[2,16,1,64,1,128]{5,3,1,0,4,2:T(8,128)(2,1)S(1)}, u32[]{:S(2)}) copy-start(bf16[2,16,1,64,1,128]{5,3,1,0,4,2:T(8,128)(2,1)S(1)} %copy.28) | copy-start | bytes 1572868
  17.5 1.5 copy-start.6
  17.6 1.4 copy-start.8
  20.7 9.1 %copy-start.15 = (s32[2,3]{1,0:T(2,128)S(1)}, s32[2,3]{1,0:T(2,128)}, u32[]{:S(2)}) copy-start(s32[2,3]{1,0:T(2,128)} %param.10) | copy-start | bytes 76
  20.8 9.1 %copy-start.16 = (s32[2]{0:T(128)S(1)}, s32[2]{0:T(128)}, u32[]{:S(2)}) copy-start(s32[2]{0:T(128)} %param.9) | copy-start | bytes 28
  22.4 22.5 %copy-start.13 = (bf16[2,3,128,128]{3,2,1,0:T(8,128)(2,1)S(1)}, bf16[2,3,128,128]{3,2,1,0:T(8,128)(2,1)}, u32[]{:S(2)}) copy-start(bf16[2,3,128,128]{3,2,1,0:T(8,128)(2,1)} %param.8) | copy-start | bytes 589828
  22.4 21.5 %all-to-all-start = ((bf16[2,1024,128]{2,0,1:T(2,128)(2,1)}), bf16[2,1024,128]{2,0,1:T(2,128)(2,1)S(1)}, u32[]{:S(2)}, u32[]{:S(2)}) async-start(bf16[2,1024,128]{2,0,1:T(2,128)(2,1)} %copy.34), calls=%async_computation | async-start | bytes 1048576 | tf_op jit(solution)/shard_map/all_to_all | solution.py:97
  44.8 0.8 copy-start.10
  44.8 1.0 copy-start.11
  47.4 1.0 copy-start.12
  54.4 18.7 %all-to-all-start.1 = ((bf16[32,64,128]{2,1,0:T(8,128)(2,1)}), bf16[32,64,128]{2,1,0:T(8,128)(2,1)}, u32[]{:S(2)}, u32[]{:S(2)}) async-start(bf16[32,64,128]{2,1,0:T(8,128)(2,1)} %fusion.9), calls=%async_computation.1 | async-start | bytes 1048576 | tf_op jit(solution)/shard_map/all_to_all | solution.py:102
  58.9 111.1 %all-reduce.12.cloned.1.call-start = ((), (), s32[]{:S(2)}) async-start(), calls=%async_computation.2 | async-start | bytes 1966080 | tf_op jit(solution)/shard_map/psum | solution.py:116
  73.2 2.2 %copy-start.1 = (bf16[2,16,1,64,1,128]{5,3,1,0,4,2:T(8,128)(2,1)S(1)}, bf16[2,16,1,64,1,128]{5,3,1,0,4,2:T(8,128)(2,1)}, u32[]{:S(2)}) copy-start(bf16[2,16,1,64,1,128]{5,3,1,0,4,2:T(8,128)(2,1)} %copy-done) | copy-start | bytes 1572868
  74.3 1.5 copy-start.3
  74.7 1.4 copy-start.5
  75.0 1.4 copy-start.7
  75.4 1.4 copy-start.9
Sparse Core Ops, SparseCore 0:
  78.6 91.4 all-reduce.11
where the time goes:
time: 183 us; the launch traced here: 181 us
  waiting for transfers between devices  111 us (61%)
  local copies, waits for them, and re-layouts  20.5 us (11%)
  between operations  18.5 us (10%)
  matrix products  13.2 us (7%)
  starting transfers between devices  12 us (7%)
  other arithmetic  5.14 us (3%)
    psum x1, waiting for transfers between devices, local(): lax.psum((local_spatial, local_temporal), 'seq')  91.6 us
    all_to_all x1, waiting for transfers between devices, local(): lax.all_to_all(grad_maps, 'seq', split_axis=0, concat_axis=1, tiled=True)  10.2 us
    all_to_all x1, waiting for transfers between devices, local(): lax.all_to_all(spatial, 'seq', split_axis=1, concat_axis=0, tiled=True)  9.38 us
    unnamed x37, local copies, waits for them, and re-layouts  9 us
    all_to_all x1, starting transfers between devices, local(): lax.all_to_all(spatial, 'seq', split_axis=1, concat_axis=0, tiled=True)  7.45 us
    slice x10, local copies, waits for them, and re-layouts, window(): view[:, row_tap // 2:row_tap // 2 + out_rows, row_tap % 2, col_tap // 2:c...  4.93 us
    all_to_all x1, starting transfers between devices, local(): lax.all_to_all(grad_maps, 'seq', split_axis=0, concat_axis=1, tiled=True)  4.5 us
    dot_general x6, matrix products, temporal_backward(): lax.dot_general(moved, dz_flat, (((0,), (0,)), ((), ())), preferred_eleme...  4.11 us
  transfers between devices with their start and end apart: 3, of which 3 were waited for; matrix products, arithmetic and copies ran while one was open for 3% of the time, Pallas kernels for 0%

commit v1 on v0

v1 whole, which is shorter than its diff:
```python
import functools

import jax
import jax.numpy as jnp
from jax import lax
from jax.experimental import pallas as pl
from jax.experimental.pallas import tpu as pltpu
from jax.sharding import PartitionSpec as P

BF16 = jnp.bfloat16
F32 = jnp.float32
MESH = pl.DeviceIdType.MESH


def kernel(
    n,
    dil_ref,
    off_ref,
    frames_ref,
    ws_ref,
    wt_ref,
    cot_ref,
    feat_ref,
    gs_ref,
    gt_ref,
    tmp,
    xcols,
    spat,
    land,
    s0,
    s1,
    act0,
    d1,
    d0,
    maps,
    back,
    wback,
    grads,
    pair_out,
    pair_in,
    chip_out,
    chip_in,
    own,
    gathered,
    send1,
    recv1,
    send2,
    recv2,
    ar_send,
    ar_recv,
):
    me = lax.axis_index("seq")
    per, height, width, ch = frames_ref.shape
    length, pix, _ = cot_ref.shape
    layers, taps = off_ref.shape
    out_h, out_w = height // 2, width // 2
    blocks = out_w // pix
    q_count = recv2.shape[0]
    q_rows = out_h // q_count
    q_devs = q_rows * blocks
    t_count = recv1.shape[0]
    t_len = length // t_count
    t_devs = t_len // per
    chips = n // 2
    core = lax.rem(me, 2)
    chip = me // 2
    partner = me + 1 - 2 * core
    sp_rows = gs_ref.shape[0]
    tap_rows = taps * ch

    def flat(x):
        if pix % 16 == 0:
            return x.reshape(-1, ch)
        return x.astype(F32).reshape(-1, ch).astype(BF16)

    def unflat(x):
        return x.reshape(-1, pix, ch)

    def delay(layer, tap):
        return jnp.minimum(off_ref[layer, tap] * dil_ref[layer], length)

    barrier = pltpu.get_barrier_semaphore()

    def greet(s, carry):
        pl.semaphore_signal(
            barrier, inc=1, device_id={"seq": lax.rem(me + s, n)}, device_id_type=MESH
        )
        return carry

    lax.fori_loop(1, n, greet, 0)

    group = tmp.shape[0]
    for g in range(group):
        tmp[g, 0:8, :] = jnp.zeros((8, ch), F32)
    for f in range(per):
        xcols[f, 0, 0] = jnp.zeros((out_w, 3 * ch), BF16)

    def spread(step, carry):
        for f in range(per):
            for g in range(group):
                r = step * group + g
                tmp[g, 8 : 8 + width, :] = frames_ref[f, r].astype(F32)
            for g in range(group):
                half = (g + 1) // 2
                row = step * (group // 2) + half
                for b in range(3):
                    xcols[f, row, (g + 1) % 2, :, b * ch : (b + 1) * ch] = tmp[
                        g, pl.ds(7 + b, out_w, stride=2), :
                    ].astype(BF16)
        return carry

    lax.fori_loop(0, height // group, spread, 0)

    def patches(f, i0, count):
        parts = [
            xcols[f, pl.ds(i0, count), 0],
            xcols[f, pl.ds(i0, count), 1],
            xcols[f, pl.ds(i0 + 1, count), 0],
        ]
        return jnp.concatenate([p.reshape(count * out_w, 3 * ch) for p in parts], axis=1)

    pl.semaphore_wait(barrier, n - 1)

    my_q = me // q_devs

    def conv(s, carry):
        q = lax.rem(my_q + 1 + s, q_count)
        for f in range(per):
            out = jnp.dot(
                patches(f, q * q_rows, q_rows), ws_ref[...], preferred_element_type=F32
            )
            spat[pl.ds(q * q_devs, q_devs), f] = unflat(out).astype(BF16)

        def send(k, c):
            j = q * q_devs + lax.rem(me + k, q_devs)

            @pl.when(j != me)
            def _():
                pltpu.make_async_remote_copy(
                    src_ref=spat.at[j],
                    dst_ref=land.at[pl.ds(me * per, per)],
                    send_sem=send1,
                    recv_sem=recv1.at[me // t_devs],
                    device_id={"seq": j},
                    device_id_type=MESH,
                ).start()

            @pl.when(j == me)
            def _():
                pltpu.make_async_copy(
                    spat.at[me],
                    land.at[pl.ds(me * per, per)],
                    recv1.at[me // t_devs],
                ).start()

            return c

        lax.fori_loop(0, q_devs, send, 0)
        return carry

    lax.fori_loop(0, q_count, conv, 0)

    def clear(t, carry):
        zero = jnp.zeros((t_len, pix, ch), BF16)
        s0[pl.ds(t * t_len, t_len)] = zero
        s1[pl.ds(t * t_len, t_len)] = zero
        d1[pl.ds(length + t * t_len, t_len)] = zero
        d0[pl.ds(length + t * t_len, t_len)] = zero
        return carry

    lax.fori_loop(0, t_count, clear, 0)
    grads[...] = jnp.zeros_like(grads)
    for layer in range(layers):
        for tap in range(taps):
            w = wt_ref[layer, tap * ch : (tap + 1) * ch, :]
            wback[layer, tap * ch : (tap + 1) * ch, :] = w.astype(F32).T.astype(BF16)

    def lagged(ref, layer, t0):
        return jnp.concatenate(
            [flat(ref[pl.ds(length + t0 - delay(layer, k), t_len)]) for k in range(taps)], axis=1
        )

    def led(ref, layer, t0):
        return jnp.concatenate(
            [flat(ref[pl.ds(t0 + delay(layer, k), t_len)]) for k in range(taps)], axis=1
        )

    def outer(x, y):
        return lax.dot_general(x, y, (((0,), (0,)), ((), ())), preferred_element_type=F32)

    base0 = sp_rows
    base1 = sp_rows + tap_rows

    def forward(t, carry):
        t0 = t * t_len
        arrived = land.at[pl.ds(t0, t_len)]
        pltpu.make_async_copy(arrived, arrived, recv1.at[t]).wait()
        state = land[pl.ds(t0, t_len)]
        s0[pl.ds(length + t0, t_len)] = state
        z = jnp.dot(lagged(s0, 0, t0), wt_ref[0], preferred_element_type=F32)
        act = unflat(jnp.tanh(z))
        act0[pl.ds(t0, t_len)] = act
        state = (state.astype(F32) + act).astype(BF16)
        s1[pl.ds(length + t0, t_len)] = state
        moved = lagged(s1, 1, t0)
        act = unflat(jnp.tanh(jnp.dot(moved, wt_ref[1], preferred_element_type=F32)))
        feat_ref[pl.ds(t0, t_len)] = (state.astype(F32) + act).astype(BF16)
        dz = (cot_ref[pl.ds(t0, t_len)].astype(F32) * (1.0 - act * act)).astype(BF16)
        d1[pl.ds(t0, t_len)] = dz
        grads[pl.ds(base1, tap_rows), :] += outer(moved, flat(dz))
        return carry

    lax.fori_loop(0, t_count, forward, 0)

    def backward(s, carry):
        t = t_count - 1 - s
        t0 = t * t_len
        state = cot_ref[pl.ds(t0, t_len)].astype(F32) + unflat(
            jnp.dot(led(d1, 1, t0), wback[1], preferred_element_type=F32)
        )
        act = act0[pl.ds(t0, t_len)]
        dz = (state * (1.0 - act * act)).astype(BF16)
        d0[pl.ds(t0, t_len)] = dz
        state = state + unflat(jnp.dot(led(d0, 0, t0), wback[0], preferred_element_type=F32))
        maps[pl.ds(t0, t_len)] = state.astype(BF16)

        def send(k, c):
            j = t * t_devs + lax.rem(me + k, t_devs)

            @pl.when(j != me)
            def _():
                pltpu.make_async_remote_copy(
                    src_ref=maps.at[pl.ds(j * per, per)],
                    dst_ref=back.at[me],
                    send_sem=send2,
                    recv_sem=recv2.at[me // q_devs],
                    device_id={"seq": j},
                    device_id_type=MESH,
                ).start()

            @pl.when(j == me)
            def _():
                pltpu.make_async_copy(
                    maps.at[pl.ds(me * per, per)], back.at[me], recv2.at[me // q_devs]
                ).start()

            return c

        lax.fori_loop(0, t_devs, send, 0)
        grads[pl.ds(base0, tap_rows), :] += outer(lagged(s0, 0, t0), flat(dz))
        return carry

    lax.fori_loop(0, t_count, backward, 0)

    def conv_grad(s, carry):
        q = lax.rem(my_q + s, q_count)
        arrived = back.at[pl.ds(q * q_devs, q_devs)]
        pltpu.make_async_copy(arrived, arrived, recv2.at[q]).wait()
        x = jnp.concatenate([patches(f, q * q_rows, q_rows) for f in range(per)], axis=0)
        g = jnp.concatenate([flat(back[pl.ds(q * q_devs, q_devs), f]) for f in range(per)], axis=0)
        grads[0:sp_rows, :] += outer(x, g)
        return carry

    lax.fori_loop(0, q_count, conv_grad, 0)

    rows = pair_out.shape[2]
    half = chips * rows

    def as_pieces(x):
        return x.reshape(chips, rows, ch)

    for c in range(2):
        pair_out[c] = as_pieces(grads[c * half : (c + 1) * half, :].astype(BF16))
    pair = pltpu.make_async_remote_copy(
        src_ref=pair_out.at[1 - core],
        dst_ref=pair_in,
        send_sem=ar_send.at[0],
        recv_sem=ar_recv.at[0],
        device_id={"seq": partner},
        device_id_type=MESH,
    )
    pair.start()
    mine = as_pieces(grads[pl.ds(pl.multiple_of(core * half, half), half), :])
    pair.wait_recv()
    chip_out[...] = (mine + pair_in[...].astype(F32)).astype(BF16)

    def scatter(k, carry):
        c = lax.rem(chip + k, chips)
        pltpu.make_async_remote_copy(
            src_ref=chip_out.at[c],
            dst_ref=chip_in.at[chip],
            send_sem=ar_send.at[1],
            recv_sem=ar_recv.at[1],
            device_id={"seq": 2 * c + core},
            device_id_type=MESH,
        ).start()
        return carry

    pltpu.make_async_copy(chip_out.at[chip], chip_in.at[chip], ar_recv.at[1]).start()
    lax.fori_loop(1, chips, scatter, 0)
    pltpu.make_async_copy(chip_in, chip_in, ar_recv.at[1]).wait()
    own[...] = jnp.sum(chip_in[...].astype(F32), axis=0).astype(BF16)

    def gather(k, carry):
        c = lax.rem(chip + k, chips)
        pltpu.make_async_remote_copy(
            src_ref=own,
            dst_ref=gathered.at[core, chip],
            send_sem=ar_send.at[2],
            recv_sem=ar_recv.at[2],
            device_id={"seq": 2 * c + core},
            device_id_type=MESH,
        ).start()
        return carry

    pltpu.make_async_copy(own, gathered.at[core, chip], ar_recv.at[2]).start()
    lax.fori_loop(1, chips, gather, 0)
    mine_all = gathered.at[core]
    pltpu.make_async_copy(mine_all, mine_all, ar_recv.at[2]).wait()
    swap = pltpu.make_async_remote_copy(
        src_ref=gathered.at[core],
        dst_ref=gathered.at[core],
        send_sem=ar_send.at[3],
        recv_sem=ar_recv.at[3],
        device_id={"seq": partner},
        device_id_type=MESH,
    )
    swap.start()
    swap.wait_recv()
    total = gathered[...].astype(F32).reshape(2 * half, ch)
    gs_ref[...] = total[:sp_rows]
    gt_ref[...] = total[sp_rows : sp_rows + gt_ref.shape[0]]

    pair.wait_send()
    swap.wait_send()
    most = spat.at[pl.ds(0, n - 1)]
    pltpu.make_async_copy(most, most, send1).wait()
    most = back.at[pl.ds(0, n - 1)]
    pltpu.make_async_copy(most, most, send2).wait()
    most = chip_out.at[pl.ds(0, chips - 1)]
    pltpu.make_async_copy(most, most, ar_send.at[1]).wait()
    pltpu.make_async_copy(most, most, ar_send.at[2]).wait()


def local(n, frames, w_spatial, w_temporal, dilations, offsets, cotangent):
    per, height, width, ch = frames.shape
    length, pix, _ = cotangent.shape
    layers, taps = offsets.shape
    out_h, out_w = height // 2, width // 2
    sp_rows, tp_rows = 9 * ch, layers * taps * ch
    unit = 16 * n
    rows = -(-(sp_rows + tp_rows) // unit) * 16
    chips = n // 2
    t_count = max(1, length * pix // 512)
    q_count = 4
    vmem = pl.BlockSpec(memory_space=pltpu.VMEM)
    smem = pl.BlockSpec(memory_space=pltpu.SMEM)
    dma = pltpu.SemaphoreType.DMA
    features, grad_spatial, grad_temporal = pl.pallas_call(
        functools.partial(kernel, n),
        out_shape=(
            jax.ShapeDtypeStruct((length, pix, ch), BF16),
            jax.ShapeDtypeStruct((sp_rows, ch), F32),
            jax.ShapeDtypeStruct((tp_rows, ch), F32),
        ),
        in_specs=[smem, smem, vmem, vmem, vmem, vmem],
        out_specs=(vmem, vmem, vmem),
        scratch_shapes=[
            pltpu.VMEM((8, width + 8, ch), F32),
            pltpu.VMEM((per, out_h + 1, 2, out_w, 3 * ch), BF16),
            pltpu.VMEM((n, per, pix, ch), BF16),
            pltpu.VMEM((length, pix, ch), BF16),
            pltpu.VMEM((2 * length, pix, ch), BF16),
            pltpu.VMEM((2 * length, pix, ch), BF16),
            pltpu.VMEM((length, pix, ch), F32),
            pltpu.VMEM((2 * length, pix, ch), BF16),
            pltpu.VMEM((2 * length, pix, ch), BF16),
            pltpu.VMEM((length, pix, ch), BF16),
            pltpu.VMEM((n, per, pix, ch), BF16),
            pltpu.VMEM((layers, taps * ch, ch), BF16),
            pltpu.VMEM((n * rows, ch), F32),
            pltpu.VMEM((2, chips, rows, ch), BF16),
            pltpu.VMEM((chips, rows, ch), BF16),
            pltpu.VMEM((chips, rows, ch), BF16),
            pltpu.VMEM((chips, rows, ch), BF16),
            pltpu.VMEM((rows, ch), BF16),
            pltpu.VMEM((2, chips, rows, ch), BF16),
            dma,
            dma((t_count,)),
            dma,
            dma((q_count,)),
            dma((4,)),
            dma((4,)),
        ],
        compiler_params=pltpu.CompilerParams(
            collective_id=0, has_side_effects=True, vmem_limit_bytes=48 * 1024 * 1024
        ),
        cost_estimate=pl.CostEstimate(
            flops=2 * (length * pix) * ch * ch * 36, bytes_accessed=8 << 20, transcendentals=0
        ),
    )(
        dilations,
        offsets,
        frames,
        w_spatial.reshape(sp_rows, ch),
        w_temporal.reshape(layers, taps * ch, ch),
        cotangent,
    )
    return (
        features,
        grad_spatial.reshape(3, 3, ch, ch),
        grad_temporal.reshape(layers, taps, ch, ch),
    )


def solution(mesh):
    in_specs = (
        P(("groups", "seq"), None, None, None),
        P(),
        P(),
        P(),
        P(),
        P("groups", "seq", None),
    )
    out_specs = (
        P("groups", "seq", None),
        P("groups", None, None, None),
        P("groups", None, None, None),
    )
    return jax.shard_map(
        functools.partial(local, mesh.shape["seq"]),
        mesh=mesh,
        in_specs=in_specs,
        out_specs=out_specs,
        check_vma=False,
    )
```

time: 183 us -> 60.9 us (0.33); the launches traced: 181 us -> 60.6 us
  waiting for transfers between devices: 111 us -> 0 us
  Pallas kernels: 0 us -> 51.8 us
  between operations: 18.5 us -> 0.65 us
  matrix products: 13.2 us -> 0 us
  local copies, waits for them, and re-layouts: 20.5 us -> 8.2 us
  starting transfers between devices: 12 us -> 0 us
  other arithmetic: 5.14 us -> 0 us
    psum x1 -> x0, waiting for transfers between devices: 91.6 us -> none  [local(): lax.psum((local_spatial, local_temporal), 'seq')]
    pallas_call x0 -> x1, Pallas kernels: none -> 51.8 us  [local(): pl.pallas_call(functools.partial(kernel, n), out_shape=(jax.ShapeDtypeStr...]
    all_to_all x2 -> x0, waiting for transfers between devices: 19.6 us -> none  [the longest x1 10.2 us: local(): lax.all_to_all(grad_maps, 'seq', split_axis=0, concat_axis=1, tiled=True)]
    dot_general x36 -> x0, matrix products: 13.2 us -> none  [the longest x6 4.11 us: temporal_backward(): lax.dot_general(moved, dz_flat, (((0,), (0,)), ((), ())), preferred_eleme...]
    all_to_all x2 -> x0, starting transfers between devices: 12 us -> none  [the longest x1 7.45 us: local(): lax.all_to_all(spatial, 'seq', split_axis=1, concat_axis=0, tiled=True)]
    slice x11 -> x0, local copies, waits for them, and re-layouts: 5.61 us -> none  [the longest x10 4.93 us: window(): view[:, row_tap // 2:row_tap // 2 + out_rows, row_tap % 2, col_tap // 2:c...]
    convert_element_type x4 -> x0, other arithmetic: 3.36 us -> none  [the longest x2 1.77 us: temporal_backward(): (grad_state * (1.0 - activ * activ)).astype(jnp.bfloat16)]
    unnamed x37 -> x15, local copies, waits for them, and re-layouts: 9 us -> 8.2 us
  transfers between devices with their start and end apart: 3 -> 0, of which waited for: 3 -> 0; matrix products, arithmetic and copies ran while one was open for 3% -> 0% of each run, Pallas kernels for 0% -> 0%
where the time goes in v1:
time: 60.9 us; the launch traced here: 60.6 us
  Pallas kernels  51.8 us (85%)
  local copies, waits for them, and re-layouts  8.2 us (13%)
  between operations  0.65 us (1%)
    pallas_call x1, Pallas kernels, local(): pl.pallas_call(functools.partial(kernel, n), out_shape=(jax.ShapeDtypeStr...  51.8 us
    unnamed x15, local copies, waits for them, and re-layouts  8.2 us

profile of v1, /device:TPU:1, one launch (start us, length us, event | category | flops | bytes accessed | tf_op | source)
XLA Modules:
  0.0 60.6 jit_solution(12680167830434684710)
XLA Ops:
  0.6 0.0 copy-start
  0.6 1.6 %copy-done = bf16[2,32,128,128]{3,2,1,0:T(8,128)(2,1)S(1)} copy-done((bf16[2,32,128,128]{3,2,1,0:T(8,128)(2,1)S(1)}, bf16[2,32,128,128]{3,2,1,0:T(8,128)(2,1)}, u32[]{:S(2)}) %copy-start) | copy-done | bytes 2097176
  2.2 0.0 copy-start.1
  2.2 1.0 %copy-done.1 = bf16[32,64,128]{2,1,0:T(8,128)(2,1)S(1)} copy-done((bf16[32,64,128]{2,1,0:T(8,128)(2,1)S(1)}, bf16[32,64,128]{2,1,0:T(8,128)(2,1)}, u32[]{:S(2)}) %copy-start.1) | copy-done | bytes 524312
  3.3 0.0 copy-start.2
  3.3 1.0 %copy-done.2 = bf16[3,3,128,128]{3,2,1,0:T(8,128)(2,1)S(1)} copy-done((bf16[3,3,128,128]{3,2,1,0:T(8,128)(2,1)S(1)}, bf16[3,3,128,128]{3,2,1,0:T(8,128)(2,1)}, u32[]{:S(2)}) %copy-start.2) | copy-done | bytes 294936
  4.2 0.0 copy-start.3
  4.2 0.9 %copy-done.3 = bf16[2,3,128,128]{3,2,1,0:T(8,128)(2,1)S(1)} copy-done((bf16[2,3,128,128]{3,2,1,0:T(8,128)(2,1)S(1)}, bf16[2,3,128,128]{3,2,1,0:T(8,128)(2,1)}, u32[]{:S(2)}) %copy-start.3) | copy-done | bytes 196632
  5.2 0.0 copy-start.4
  5.2 0.7 %copy-done.4 = s32[2,3]{1,0:T(2,128)S(1)} copy-done((s32[2,3]{1,0:T(2,128)S(1)}, s32[2,3]{1,0:T(2,128)}, u32[]{:S(2)}) %copy-start.4) | copy-done | bytes 48
  5.8 0.0 copy-start.5
  5.8 0.7 %copy-done.5 = s32[2]{0:T(128)S(1)} copy-done((s32[2]{0:T(128)S(1)}, s32[2]{0:T(128)}, u32[]{:S(2)}) %copy-start.5) | copy-done | bytes 32
  6.5 51.8 %shard_map.85 = (bf16[32,64,128]{2,1,0:T(8,128)(2,1)S(1)}, f32[1152,128]{1,0:T(8,128)S(1)}, f32[768,128]{1,0:T(8,128)S(1)}) custom-call(s32[2]{0:T(128)S(1)} %copy-done.5, s32[2,3]{1,0:T(2,128)S(1)} %copy-done.4, bf16[2,32,128,128]{3,2,1,0:T(8,128)(2,1)S(1)} %copy-done, bf16[1152,128]{1,0:T(8,128)(2,1)S(1)} %bitcast.6, bf16[2,384,128]{2,1,0:T(8,128)(2,1)S(1)} %bitcast.7, ...), custom_call_target="tpu_custom_call" | custom-call | flops 2415919104 | bytes 8388608 | tf_op jit(solution)/shard_map/pallas_call | solution.py:359
  58.3 0.8 %copy.12 = bf16[32,64,128]{2,1,0:T(8,128)(2,1)} copy(bf16[32,64,128]{2,1,0:T(8,128)(2,1)S(1)} %get-tuple-element.12) | data formatting | bytes 1048576
  59.1 0.8 %copy.13 = f32[3,3,128,128]{3,2,1,0:T(8,128)} copy(f32[3,3,128,128]{3,2,1,0:T(8,128)S(1)} %bitcast.4) | data formatting | bytes 1179648
  59.9 0.7 %copy.14 = f32[2,3,128,128]{3,2,1,0:T(8,128)} copy(f32[2,3,128,128]{3,2,1,0:T(8,128)S(1)} %bitcast.5) | data formatting | bytes 786432
Async XLA Ops:
  0.6 1.6 %copy-start = (bf16[2,32,128,128]{3,2,1,0:T(8,128)(2,1)S(1)}, bf16[2,32,128,128]{3,2,1,0:T(8,128)(2,1)}, u32[]{:S(2)}) copy-start(bf16[2,32,128,128]{3,2,1,0:T(8,128)(2,1)} %frames_ref.1) | copy-start | bytes 6291460
  2.2 1.0 %copy-start.1 = (bf16[32,64,128]{2,1,0:T(8,128)(2,1)S(1)}, bf16[32,64,128]{2,1,0:T(8,128)(2,1)}, u32[]{:S(2)}) copy-start(bf16[32,64,128]{2,1,0:T(8,128)(2,1)} %cot_ref.1) | copy-start | bytes 1572868
  3.3 1.0 %copy-start.2 = (bf16[3,3,128,128]{3,2,1,0:T(8,128)(2,1)S(1)}, bf16[3,3,128,128]{3,2,1,0:T(8,128)(2,1)}, u32[]{:S(2)}) copy-start(bf16[3,3,128,128]{3,2,1,0:T(8,128)(2,1)} %param.7) | copy-start | bytes 884740
  4.2 0.9 %copy-start.3 = (bf16[2,3,128,128]{3,2,1,0:T(8,128)(2,1)S(1)}, bf16[2,3,128,128]{3,2,1,0:T(8,128)(2,1)}, u32[]{:S(2)}) copy-start(bf16[2,3,128,128]{3,2,1,0:T(8,128)(2,1)} %param.8) | copy-start | bytes 589828
  5.2 0.7 %copy-start.4 = (s32[2,3]{1,0:T(2,128)S(1)}, s32[2,3]{1,0:T(2,128)}, u32[]{:S(2)}) copy-start(s32[2,3]{1,0:T(2,128)} %off_ref.1) | copy-start | bytes 76
  5.8 0.7 %copy-start.5 = (s32[2]{0:T(128)S(1)}, s32[2]{0:T(128)}, u32[]{:S(2)}) copy-start(s32[2]{0:T(128)} %dil_ref.1) | copy-start | bytes 28

commit v2 on v0

v2 whole, which is shorter than its diff:
```python
import functools

import jax
import jax.numpy as jnp
from jax import lax
from jax.experimental import pallas as pl
from jax.experimental.pallas import tpu as pltpu
from jax.sharding import PartitionSpec as P

BF16 = jnp.bfloat16
F32 = jnp.float32
MESH = pl.DeviceIdType.MESH
PARTS = 4


def remote(src, dst, send, recv, to):
    return pltpu.make_async_remote_copy(
        src_ref=src,
        dst_ref=dst,
        send_sem=send,
        recv_sem=recv,
        device_id={"seq": to},
        device_id_type=MESH,
    )


def drain(ref, sem):
    pltpu.make_async_copy(ref, ref, sem).wait()


class Reduce:
    def __init__(self, n, out, total, pair_out, pair_in, chip_out, chip_in, own, gathered, send, recv):
        self.total, self.pair_out, self.pair_in = total, pair_out, pair_in
        self.chip_out, self.chip_in, self.own = chip_out, chip_in, own
        self.gathered, self.send, self.recv, self.out = gathered, send, recv, out
        self.chips = n // 2
        me = lax.axis_index("seq")
        self.core, self.chip = lax.rem(me, 2), me // 2
        self.partner = me + 1 - 2 * self.core
        self.rows, self.ch = own.shape
        self.half = self.chips * self.rows
        self.pair = remote(
            pair_out.at[1 - self.core], pair_in, send.at[0], recv.at[0], self.partner
        )
        self.swap = remote(
            gathered.at[self.core], gathered.at[self.core], send.at[3], recv.at[3], self.partner
        )

    def pieces(self, x):
        return x.reshape(self.chips, self.rows, self.ch)

    def chips_loop(self, src_of, dst, hop):
        def step(k, carry):
            c = lax.rem(self.chip + k, self.chips)
            remote(
                src_of(c), dst, self.send.at[hop], self.recv.at[hop], 2 * c + self.core
            ).start()
            return carry

        lax.fori_loop(1, self.chips, step, 0)

    def start(self):
        for c in range(2):
            part = self.total[c * self.half : (c + 1) * self.half, :]
            self.pair_out[c] = self.pieces(part.astype(BF16))
        self.pair.start()

    def scatter(self):
        at = pl.multiple_of(self.core * self.half, self.half)
        mine = self.pieces(self.total[pl.ds(at, self.half), :])
        self.pair.wait_recv()
        self.chip_out[...] = (mine + self.pair_in[...].astype(F32)).astype(BF16)
        dst = self.chip_in.at[self.chip]
        self.chips_loop(lambda c: self.chip_out.at[c], dst, 1)
        pltpu.make_async_copy(self.chip_out.at[self.chip], dst, self.recv.at[1]).start()

    def gather(self):
        drain(self.chip_in, self.recv.at[1])
        self.own[...] = jnp.sum(self.chip_in[...].astype(F32), axis=0).astype(BF16)
        dst = self.gathered.at[self.core, self.chip]
        self.chips_loop(lambda c: self.own, dst, 2)
        pltpu.make_async_copy(self.own, dst, self.recv.at[2]).start()

    def exchange(self):
        drain(self.gathered.at[self.core], self.recv.at[2])
        self.swap.start()
        self.store(self.core).start()

    def finish(self):
        self.swap.wait_recv()
        self.store(1 - self.core).start()

    def store(self, side):
        return pltpu.make_async_copy(self.gathered.at[side], self.out.at[side], self.recv.at[4])

    def sent(self):
        self.pair.wait_send()
        self.swap.wait_send()
        most = self.chip_out.at[pl.ds(0, self.chips - 1)]
        drain(most, self.send.at[1])
        drain(most, self.send.at[2])
        drain(self.gathered, self.recv.at[4])


def kernel(
    n,
    dil_ref,
    off_ref,
    frames_hbm,
    ws_hbm,
    wt_hbm,
    cot_hbm,
    feat_hbm,
    gs_hbm,
    gt_hbm,
    feat_ref,
    frames_ref,
    ws_ref,
    wt_ref,
    cot_ref,
    tmp,
    xcols,
    spat,
    land,
    s0,
    s1,
    act0,
    d1,
    d0,
    maps,
    back,
    wback,
    sum_s,
    sum_t,
    *rest,
):
    red_s = Reduce(n, gs_hbm, sum_s, *rest[0:8])
    red_t = Reduce(n, gt_hbm, sum_t, *rest[8:16])
    send1, recv1, send2, recv2, load = rest[16:]
    me = lax.axis_index("seq")
    per, height, width, ch = frames_ref.shape
    length, pix, _ = cot_ref.shape
    layers, taps = off_ref.shape
    parts, _, _, pp, _ = spat.shape
    out_h, out_w = height // 2, width // 2
    cw = out_w // parts
    q_count = 4
    q_rows = out_h // q_count
    q_devs = n // q_count
    g_count = max(1, per * out_h * cw // 512)
    g_rows, g_devs = out_h // g_count, n // g_count
    t_count = max(1, length * pp // 512)
    t_len = length // t_count
    sp_rows = ws_ref.shape[0]
    tap_rows = taps * ch

    fetch = [
        pltpu.make_async_copy(frames_hbm.at[f], frames_ref.at[f], load.at[f]) for f in range(per)
    ]
    fetch += [
        pltpu.make_async_copy(a, b, load.at[per + i])
        for i, (a, b) in enumerate([(ws_hbm, ws_ref), (wt_hbm, wt_ref), (cot_hbm, cot_ref)])
    ]
    for copy in fetch:
        copy.start()

    def flat(x):
        if pp % 16 == 0:
            return x.reshape(-1, x.shape[-1])
        return x.astype(F32).reshape(-1, x.shape[-1]).astype(BF16)

    def unflat(x):
        return x.reshape(-1, pp, ch)

    def delay(layer, tap):
        return jnp.minimum(off_ref[layer, tap] * dil_ref[layer], length)

    barrier = pltpu.get_barrier_semaphore()

    def greet(s, carry):
        pl.semaphore_signal(
            barrier, inc=1, device_id={"seq": lax.rem(me + s, n)}, device_id_type=MESH
        )
        return carry

    lax.fori_loop(1, n, greet, 0)

    group = tmp.shape[0]
    for g in range(group):
        tmp[g, 0:8, :] = jnp.zeros((8, ch), F32)
    for f in range(per):
        xcols[f, 0, 0] = jnp.zeros((parts, cw, 3 * ch), BF16)

    for f in range(per):
        fetch[f].wait()

        def spread(step, carry):
            for g in range(group):
                tmp[g, 8 : 8 + width, :] = frames_ref[f, step * group + g].astype(F32)
            for g in range(group):
                row = step * (group // 2) + (g + 1) // 2
                for b in range(3):
                    col = tmp[g, pl.ds(7 + b, out_w, stride=2), :].astype(BF16)
                    xcols[f, row, (g + 1) % 2, :, :, b * ch : (b + 1) * ch] = col.reshape(
                        parts, cw, ch
                    )
            return carry

        lax.fori_loop(0, height // group, spread, 0)

    def row_taps(f, i0, count, *part):
        views = [
            xcols[(f, pl.ds(i0, count), 0, *part)],
            xcols[(f, pl.ds(i0, count), 1, *part)],
            xcols[(f, pl.ds(i0 + 1, count), 0, *part)],
        ]
        return jnp.concatenate([v.reshape(-1, 3 * ch) for v in views], axis=1)

    fetch[per].wait()
    pl.semaphore_wait(barrier, n - 1)

    my_q = me // q_devs
    mine = pl.ds(me * per, per)

    def send_map(h, j):
        @pl.when(j != me)
        def _():
            remote(spat.at[h, j], land.at[h, mine], send1, recv1.at[h], j).start()

        @pl.when(j == me)
        def _():
            pltpu.make_async_copy(spat.at[h, j], land.at[h, mine], recv1.at[h]).start()

    def conv(s, carry):
        q = lax.rem(my_q + 1 + s, q_count)
        devs = pl.ds(q * q_devs, q_devs)
        for f in range(per):
            out = jnp.dot(
                row_taps(f, q * q_rows, q_rows), ws_ref[...], preferred_element_type=F32
            )
            out = out.reshape(q_devs, parts, pp, ch).astype(BF16)
            for h in range(parts):
                spat[h, devs, f] = out[:, h]

        def first(k, c):
            send_map(0, q * q_devs + lax.rem(me + k, q_devs))
            return c

        lax.fori_loop(0, q_devs, first, 0)
        return carry

    lax.fori_loop(0, q_count, conv, 0)

    def later(i, carry):
        send_map(1 + i // n, lax.rem(me + 1 + lax.rem(i, n), n))
        return carry

    lax.fori_loop(0, (parts - 1) * n, later, 0)

    fetch[per + 1].wait()
    fetch[per + 2].wait()

    def clear(t, carry):
        zero = jnp.zeros((t_len, pp, ch), BF16)
        s0[pl.ds(t * t_len, t_len)] = zero
        s1[pl.ds(t * t_len, t_len)] = zero
        d1[pl.ds(length + t * t_len, t_len)] = zero
        d0[pl.ds(length + t * t_len, t_len)] = zero
        return carry

    lax.fori_loop(0, t_count, clear, 0)
    sum_s[...] = jnp.zeros_like(sum_s)
    sum_t[...] = jnp.zeros_like(sum_t)
    for layer in range(layers):
        for tap in range(taps):
            w = wt_ref[layer, tap * ch : (tap + 1) * ch, :]
            wback[layer, tap * ch : (tap + 1) * ch, :] = w.astype(F32).T.astype(BF16)

    def lagged(ref, layer, t0):
        return jnp.concatenate(
            [flat(ref[pl.ds(length + t0 - delay(layer, k), t_len)]) for k in range(taps)], axis=1
        )

    def led(ref, layer, t0):
        return jnp.concatenate(
            [flat(ref[pl.ds(t0 + delay(layer, k), t_len)]) for k in range(taps)], axis=1
        )

    def outer(x, y):
        return lax.dot_general(x, y, (((0,), (0,)), ((), ())), preferred_element_type=F32)

    def steps(count, body):
        if count == 1:
            body(0)
        else:
            lax.fori_loop(0, count, lambda t, c: (body(t), c)[1], 0)

    def temporal(h, carry):
        cols = pl.ds(pl.multiple_of(h * pp, pp), pp)
        drain(land.at[h], recv1.at[h])

        def forward(t):
            t0 = t * t_len
            state = land[h, pl.ds(t0, t_len)]
            s0[pl.ds(length + t0, t_len)] = state
            z = jnp.dot(lagged(s0, 0, t0), wt_ref[0], preferred_element_type=F32)
            act = unflat(jnp.tanh(z))
            act0[pl.ds(t0, t_len)] = act
            state = (state.astype(F32) + act).astype(BF16)
            s1[pl.ds(length + t0, t_len)] = state
            moved = lagged(s1, 1, t0)
            act = unflat(jnp.tanh(jnp.dot(moved, wt_ref[1], preferred_element_type=F32)))
            feat_ref[pl.ds(t0, t_len), cols] = (state.astype(F32) + act).astype(BF16)
            cot = cot_ref[pl.ds(t0, t_len), cols].astype(F32)
            dz = (cot * (1.0 - act * act)).astype(BF16)
            d1[pl.ds(t0, t_len)] = dz
            sum_t[tap_rows : 2 * tap_rows, :] += outer(moved, flat(dz))

        steps(t_count, forward)

        def backward(s):
            t0 = (t_count - 1 - s) * t_len
            state = cot_ref[pl.ds(t0, t_len), cols].astype(F32) + unflat(
                jnp.dot(led(d1, 1, t0), wback[1], preferred_element_type=F32)
            )
            act = act0[pl.ds(t0, t_len)]
            dz = (state * (1.0 - act * act)).astype(BF16)
            d0[pl.ds(t0, t_len)] = dz
            state = state + unflat(jnp.dot(led(d0, 0, t0), wback[0], preferred_element_type=F32))
            maps[h, pl.ds(t0, t_len)] = state.astype(BF16)
            sum_t[0:tap_rows, :] += outer(lagged(s0, 0, t0), flat(dz))

        steps(t_count, backward)

        def send(k, c):
            j = lax.rem(me + k, n)
            remote(
                maps.at[h, pl.ds(j * per, per)], back.at[h, me], send2, recv2.at[h], j
            ).start()
            return c

        lax.fori_loop(1, n, send, 0)
        pltpu.make_async_copy(maps.at[h, mine], back.at[h, me], recv2.at[h]).start()
        return carry

    lax.fori_loop(0, parts, temporal, 0)

    def conv_grad(h):
        drain(back.at[h], recv2.at[h])

        def rows(s):
            i0 = s * g_rows
            x = jnp.concatenate([row_taps(f, i0, g_rows, h) for f in range(per)], axis=0)
            g = [flat(back[h, pl.ds(s * g_devs, g_devs), f]) for f in range(per)]
            sum_s[0:sp_rows, :] += outer(x, jnp.concatenate(g, axis=0))

        steps(g_count, rows)

    store = pltpu.make_async_copy(feat_ref, feat_hbm, load.at[0])
    store.start()
    hops = [red_t.start, red_t.scatter, red_t.gather, red_t.exchange]
    hops[0]()
    for h in range(parts):
        conv_grad(h)
        if h + 1 < min(parts, len(hops)):
            hops[h + 1]()
    red_s.start()
    for hop in hops[max(1, min(parts, len(hops))) :]:
        hop()
    red_s.scatter()
    red_t.finish()
    red_s.gather()
    red_s.exchange()
    red_s.finish()

    store.wait()
    red_s.sent()
    red_t.sent()
    for ref, sem in ((land, send1), (back, send2)):
        for h in range(parts):
            drain(spat.at[h, pl.ds(0, n - 1)], sem)


def reduce_scratch(n, total_rows, ch):
    chips = n // 2
    rows = -(-total_rows // (16 * n)) * 16
    dma = pltpu.SemaphoreType.DMA
    return rows * n, [
        pltpu.VMEM((2, chips, rows, ch), BF16),
        pltpu.VMEM((chips, rows, ch), BF16),
        pltpu.VMEM((chips, rows, ch), BF16),
        pltpu.VMEM((chips, rows, ch), BF16),
        pltpu.VMEM((rows, ch), BF16),
        pltpu.VMEM((2, chips, rows, ch), BF16),
        dma((4,)),
        dma((5,)),
    ]


def local(n, frames, w_spatial, w_temporal, dilations, offsets, cotangent):
    per, height, width, ch = frames.shape
    length, pix, _ = cotangent.shape
    layers, taps = offsets.shape
    out_h, out_w = height // 2, width // 2
    sp_rows, tp_rows = 9 * ch, layers * taps * ch
    parts = PARTS if pix == out_w and pix % (16 * PARTS) == 0 else 1
    pp = pix // parts
    pad_s, red_s = reduce_scratch(n, sp_rows, ch)
    pad_t, red_t = reduce_scratch(n, tp_rows, ch)
    smem = pl.BlockSpec(memory_space=pltpu.SMEM)
    hbm = pl.BlockSpec(memory_space=pltpu.HBM)
    dma = pltpu.SemaphoreType.DMA
    features, grad_spatial, grad_temporal = pl.pallas_call(
        functools.partial(kernel, n),
        out_shape=(
            jax.ShapeDtypeStruct((length, pix, ch), BF16),
            jax.ShapeDtypeStruct((2, n // 2, pad_s // n, ch), BF16),
            jax.ShapeDtypeStruct((2, n // 2, pad_t // n, ch), BF16),
        ),
        in_specs=[smem, smem, hbm, hbm, hbm, hbm],
        out_specs=(hbm, hbm, hbm),
        scratch_shapes=[
            pltpu.VMEM(cotangent.shape, BF16),
            pltpu.VMEM(frames.shape, BF16),
            pltpu.VMEM((sp_rows, ch), BF16),
            pltpu.VMEM((layers, taps * ch, ch), BF16),
            pltpu.VMEM(cotangent.shape, BF16),
            pltpu.VMEM((8, width + 8, ch), F32),
            pltpu.VMEM((per, out_h + 1, 2, parts, out_w // parts, 3 * ch), BF16),
            pltpu.VMEM((parts, n, per, pp, ch), BF16),
            pltpu.VMEM((parts, length, pp, ch), BF16),
            pltpu.VMEM((2 * length, pp, ch), BF16),
            pltpu.VMEM((2 * length, pp, ch), BF16),
            pltpu.VMEM((length, pp, ch), F32),
            pltpu.VMEM((2 * length, pp, ch), BF16),
            pltpu.VMEM((2 * length, pp, ch), BF16),
            pltpu.VMEM((parts, length, pp, ch), BF16),
            pltpu.VMEM((parts, n, per, pp, ch), BF16),
            pltpu.VMEM((layers, taps * ch, ch), BF16),
            pltpu.VMEM((pad_s, ch), F32),
            pltpu.VMEM((pad_t, ch), F32),
            *red_s,
            *red_t,
            dma,
            dma((parts,)),
            dma,
            dma((parts,)),
            dma((per + 3,)),
        ],
        compiler_params=pltpu.CompilerParams(
            collective_id=0, has_side_effects=True, vmem_limit_bytes=60 * 1024 * 1024
        ),
        cost_estimate=pl.CostEstimate(
            flops=2 * (length * pix) * ch * ch * 36, bytes_accessed=8 << 20, transcendentals=0
        ),
    )(
        dilations,
        offsets,
        frames,
        w_spatial.reshape(sp_rows, ch),
        w_temporal.reshape(layers, taps * ch, ch),
        cotangent,
    )
    return (
        features,
        grad_spatial.reshape(-1, ch)[:sp_rows].astype(F32).reshape(3, 3, ch, ch),
        grad_temporal.reshape(-1, ch)[:tp_rows].astype(F32).reshape(layers, taps, ch, ch),
    )


def solution(mesh):
    in_specs = (
        P(("groups", "seq"), None, None, None),
        P(),
        P(),
        P(),
        P(),
        P("groups", "seq", None),
    )
    out_specs = (
        P("groups", "seq", None),
        P("groups", None, None, None),
        P("groups", None, None, None),
    )
    return jax.shard_map(
        functools.partial(local, mesh.shape["seq"]),
        mesh=mesh,
        in_specs=in_specs,
        out_specs=out_specs,
        check_vma=False,
    )
```

time: 183 us -> 57 us (0.31); the launches traced: 181 us -> 56.8 us
  waiting for transfers between devices: 111 us -> 0 us
  Pallas kernels: 0 us -> 51.7 us
  local copies, waits for them, and re-layouts: 20.5 us -> 1.84 us
  between operations: 18.5 us -> 0.65 us
  matrix products: 13.2 us -> 0 us
  starting transfers between devices: 12 us -> 0 us
  other arithmetic: 5.14 us -> 2.56 us
    psum x1 -> x0, waiting for transfers between devices: 91.6 us -> none  [local(): lax.psum((local_spatial, local_temporal), 'seq')]
    pallas_call x0 -> x1, Pallas kernels: none -> 51.7 us  [local(): pl.pallas_call(functools.partial(kernel, n), out_shape=(jax.ShapeDtypeStr...]
    all_to_all x2 -> x0, waiting for transfers between devices: 19.6 us -> none  [the longest x1 10.2 us: local(): lax.all_to_all(grad_maps, 'seq', split_axis=0, concat_axis=1, tiled=True)]
    dot_general x36 -> x0, matrix products: 13.2 us -> none  [the longest x6 4.11 us: temporal_backward(): lax.dot_general(moved, dz_flat, (((0,), (0,)), ((), ())), preferred_eleme...]
    all_to_all x2 -> x0, starting transfers between devices: 12 us -> none  [the longest x1 7.45 us: local(): lax.all_to_all(spatial, 'seq', split_axis=1, concat_axis=0, tiled=True)]
    unnamed x37 -> x3, local copies, waits for them, and re-layouts: 9 us -> 0.8 us
    slice x11 -> x1, local copies, waits for them, and re-layouts: 5.61 us -> 1.04 us  [local(): grad_spatial.reshape(-1, ch)[:sp_rows].astype(F32).reshape(3, 3, ch, ch)]
  transfers between devices with their start and end apart: 3 -> 0, of which waited for: 3 -> 0; matrix products, arithmetic and copies ran while one was open for 3% -> 0% of each run, Pallas kernels for 0% -> 0%
where the time goes in v2:
time: 57 us; the launch traced here: 56.8 us
  Pallas kernels  51.7 us (91%)
  other arithmetic  2.56 us (4%)
  local copies, waits for them, and re-layouts  1.84 us (3%)
  between operations  0.65 us (1%)
    pallas_call x1, Pallas kernels, local(): pl.pallas_call(functools.partial(kernel, n), out_shape=(jax.ShapeDtypeStr...  51.7 us
    convert_element_type x1, other arithmetic, local(): grad_temporal.reshape(-1, ch)[:tp_rows].astype(F32)  1.7 us

profile of v2, /device:TPU:1, one launch (start us, length us, event | category | flops | bytes accessed | tf_op | source)
XLA Modules:
  0.0 56.8 jit_solution(9185912036122722539)
XLA Ops:
  0.6 51.7 %shard_map.85 = (bf16[32,64,128]{2,1,0:T(8,128)(2,1)}, bf16[2,8,80,128]{3,2,1,0:T(8,128)(2,1)}, bf16[2,8,48,128]{3,2,1,0:T(8,128)(2,1)}) custom-call(s32[2]{0:T(128)} %dil_ref.1, s32[2,3]{1,0:T(2,128)} %off_ref.1, bf16[2,32,128,128]{3,2,1,0:T(8,128)(2,1)} %frames_hbm.1, bf16[1152,128]{1,0:T(8,128)(2,1)} %bitcast.10, bf16[2,384,128]{2,1,0:T(8,128)(2,1)} %bitcast.11, ...), custom_call_target="tpu_custom_call" | custom-call | flops 2415919104 | bytes 8388608 | tf_op jit(solution)/shard_map/pallas_call | solution.py:413
  52.3 0.0 copy-start
  52.4 1.0 %slice.4 = bf16[1152,128]{1,0:T(8,128)(2,1)S(1)} slice(bf16[1280,128]{1,0:T(8,128)(2,1)} %bitcast.8), slice={[0:1152], [0:128]} | slice | bytes 589824 | tf_op jit(solution)/shard_map/slice | solution.py:466
  53.4 0.9 %convert.2 = f32[3,3,128,128]{3,2,1,0:T(8,128)} convert(bf16[3,3,128,128]{3,2,1,0:T(8,128)(2,1)S(1)} %bitcast.7) | non-fusion elementwise | flops 147456 | bytes 884736 | tf_op jit(solution)/shard_map/reshape | solution.py:466
  54.3 1.7 %convert.3 = f32[2,3,128,128]{3,2,1,0:T(8,128)} convert(bf16[2,3,128,128]{3,2,1,0:T(8,128)(2,1)} %bitcast.9) | non-fusion elementwise | flops 98304 | bytes 589824 | tf_op jit(solution)/shard_map/convert_element_type | solution.py:467
  56.0 0.0 copy-done
  56.0 0.8 %copy.10 = bf16[32,64,128]{2,1,0:T(8,128)(2,1)} copy(bf16[32,64,128]{2,1,0:T(8,128)(2,1)S(1)} %copy-done) | data formatting | bytes 1048576
Async XLA Ops:
  52.3 3.6 %copy-start = (bf16[32,64,128]{2,1,0:T(8,128)(2,1)S(1)}, bf16[32,64,128]{2,1,0:T(8,128)(2,1)}, u32[]{:S(2)}) copy-start(bf16[32,64,128]{2,1,0:T(8,128)(2,1)} %get-tuple-element.12) | copy-start | bytes 1572868

commit v3 on v2

--- a/solution.py
+++ b/solution.py
@@ -84,14 +84,22 @@
     def exchange(self):
         drain(self.gathered.at[self.core], self.recv.at[2])
         self.swap.start()
-        self.store(self.core).start()
+        self.widen(self.core)
 
     def finish(self):
         self.swap.wait_recv()
-        self.store(1 - self.core).start()
-
-    def store(self, side):
-        return pltpu.make_async_copy(self.gathered.at[side], self.out.at[side], self.recv.at[4])
+        self.widen(1 - self.core)
+        self.store().start()
+
+    def widen(self, side):
+        at = pl.multiple_of(side * self.half, self.half)
+        self.total[pl.ds(at, self.half), :] = (
+            self.gathered[side].astype(F32).reshape(self.half, self.ch)
+        )
+
+    def store(self):
+        held = self.total.at[pl.ds(0, self.out.shape[0])]
+        return pltpu.make_async_copy(held, self.out, self.recv.at[4])
 
     def sent(self):
         self.pair.wait_send()
@@ -99,7 +107,7 @@
         most = self.chip_out.at[pl.ds(0, self.chips - 1)]
         drain(most, self.send.at[1])
         drain(most, self.send.at[2])
-        drain(self.gathered, self.recv.at[4])
+        self.store().wait()
 
 
 def kernel(
@@ -132,6 +140,8 @@
     wback,
     sum_s,
     sum_t,
+    turned_s,
+    turned_t,
     *rest,
 ):
     red_s = Reduce(n, gs_hbm, sum_s, *rest[0:8])
@@ -234,13 +244,12 @@
     def conv(s, carry):
         q = lax.rem(my_q + 1 + s, q_count)
         devs = pl.ds(q * q_devs, q_devs)
+        x = jnp.concatenate([row_taps(f, q * q_rows, q_rows) for f in range(per)], axis=0)
+        out = jnp.dot(x, ws_ref[...], preferred_element_type=F32)
+        out = out.reshape(per, q_devs, parts, pp, ch).astype(BF16)
         for f in range(per):
-            out = jnp.dot(
-                row_taps(f, q * q_rows, q_rows), ws_ref[...], preferred_element_type=F32
-            )
-            out = out.reshape(q_devs, parts, pp, ch).astype(BF16)
             for h in range(parts):
-                spat[h, devs, f] = out[:, h]
+                spat[h, devs, f] = out[f, :, h]
 
         def first(k, c):
             send_map(0, q * q_devs + lax.rem(me + k, q_devs))
@@ -269,8 +278,9 @@
         return carry
 
     lax.fori_loop(0, t_count, clear, 0)
-    sum_s[...] = jnp.zeros_like(sum_s)
-    sum_t[...] = jnp.zeros_like(sum_t)
+    turned_s[...] = jnp.zeros_like(turned_s)
+    turned_t[...] = jnp.zeros_like(turned_t)
+    sum_s[sp_rows:, :] = jnp.zeros((sum_s.shape[0] - sp_rows, ch), F32)
     for layer in range(layers):
         for tap in range(taps):
             w = wt_ref[layer, tap * ch : (tap + 1) * ch, :]
@@ -314,7 +324,7 @@
             cot = cot_ref[pl.ds(t0, t_len), cols].astype(F32)
             dz = (cot * (1.0 - act * act)).astype(BF16)
             d1[pl.ds(t0, t_len)] = dz
-            sum_t[tap_rows : 2 * tap_rows, :] += outer(moved, flat(dz))
+            turned_t[1] += outer(flat(dz), moved)
 
         steps(t_count, forward)
 
@@ -328,7 +338,7 @@
             d0[pl.ds(t0, t_len)] = dz
             state = state + unflat(jnp.dot(led(d0, 0, t0), wback[0], preferred_element_type=F32))
             maps[h, pl.ds(t0, t_len)] = state.astype(BF16)
-            sum_t[0:tap_rows, :] += outer(lagged(s0, 0, t0), flat(dz))
+            turned_t[0] += outer(flat(dz), lagged(s0, 0, t0))
 
         steps(t_count, backward)
 
@@ -352,18 +362,24 @@
             i0 = s * g_rows
             x = jnp.concatenate([row_taps(f, i0, g_rows, h) for f in range(per)], axis=0)
             g = [flat(back[h, pl.ds(s * g_devs, g_devs), f]) for f in range(per)]
-            sum_s[0:sp_rows, :] += outer(x, jnp.concatenate(g, axis=0))
+            turned_s[...] += outer(jnp.concatenate(g, axis=0), x)
 
         steps(g_count, rows)
 
     store = pltpu.make_async_copy(feat_ref, feat_hbm, load.at[0])
     store.start()
+    for layer in range(layers):
+        for k in range(taps):
+            at = layer * tap_rows + k * ch
+            sum_t[at : at + ch, :] = turned_t[layer, :, k * ch : (k + 1) * ch].T
     hops = [red_t.start, red_t.scatter, red_t.gather, red_t.exchange]
     hops[0]()
     for h in range(parts):
         conv_grad(h)
         if h + 1 < min(parts, len(hops)):
             hops[h + 1]()
+    for at in range(0, sp_rows, ch):
+        sum_s[at : at + ch, :] = turned_s[:, at : at + ch].T
     red_s.start()
     for hop in hops[max(1, min(parts, len(hops))) :]:
         hop()
@@ -395,6 +411,30 @@
         dma((4,)),
         dma((5,)),
     ]
+
+
+def hand_over(*arrays):
+    count = len(arrays)
+
+    def body(*refs):
+        sems = refs[2 * count]
+        copies = [
+            pltpu.make_async_copy(refs[i], refs[count + i], sems.at[i]) for i in range(count)
+        ]
+        for copy in copies:
+            copy.start()
+        for copy in copies:
+            copy.wait()
+
+    hbm = pl.BlockSpec(memory_space=pltpu.HBM)
+    return pl.pallas_call(
+        body,
+        out_shape=tuple(jax.ShapeDtypeStruct(a.shape, a.dtype) for a in arrays),
+        in_specs=[hbm] * count,
+        out_specs=(hbm,) * count,
+        scratch_shapes=[pltpu.SemaphoreType.DMA((count,))],
+        compiler_params=pltpu.CompilerParams(vmem_limit_bytes=60 * 1024 * 1024),
+    )(*arrays)
 
 
 def local(n, frames, w_spatial, w_temporal, dilations, offsets, cotangent):
@@ -414,8 +454,8 @@
         functools.partial(kernel, n),
         out_shape=(
             jax.ShapeDtypeStruct((length, pix, ch), BF16),
-            jax.ShapeDtypeStruct((2, n // 2, pad_s // n, ch), BF16),
-            jax.ShapeDtypeStruct((2, n // 2, pad_t // n, ch), BF16),
+            jax.ShapeDtypeStruct((sp_rows, ch), F32),
+            jax.ShapeDtypeStruct((tp_rows, ch), F32),
         ),
         in_specs=[smem, smem, hbm, hbm, hbm, hbm],
         out_specs=(hbm, hbm, hbm),
@@ -439,6 +479,8 @@
             pltpu.VMEM((layers, taps * ch, ch), BF16),
             pltpu.VMEM((pad_s, ch), F32),
             pltpu.VMEM((pad_t, ch), F32),
+            pltpu.VMEM((ch, sp_rows), F32),
+            pltpu.VMEM((layers, ch, taps * ch), F32),
             *red_s,
             *red_t,
             dma,
@@ -461,10 +503,11 @@
         w_temporal.reshape(layers, taps * ch, ch),
         cotangent,
     )
+    features, grad_spatial, grad_temporal = hand_over(features, grad_spatial, grad_temporal)
     return (
         features,
-        grad_spatial.reshape(-1, ch)[:sp_rows].astype(F32).reshape(3, 3, ch, ch),
-        grad_temporal.reshape(-1, ch)[:tp_rows].astype(F32).reshape(layers, taps, ch, ch),
+        grad_spatial.reshape(3, 3, ch, ch),
+        grad_temporal.reshape(layers, taps, ch, ch),
     )
 
 

time: 57 us -> 99.2 us (1.74)
  Pallas kernels: 51.7 us -> 98.4 us
  other arithmetic: 2.56 us -> 0 us
  local copies, waits for them, and re-layouts: 1.84 us -> 0 us
    pallas_call x0 -> x1, Pallas kernels: none -> 46.8 us  [hand_over(): pl.pallas_call(body, out_shape=tuple((jax.ShapeDtypeStruct(a.shape, a.dty...]
    convert_element_type x1 -> x0, other arithmetic: 1.7 us -> none  [local(): grad_temporal.reshape(-1, ch)[:tp_rows].astype(F32)]
    slice x1 -> x0, local copies, waits for them, and re-layouts: 1.04 us -> none  [local(): grad_spatial.reshape(-1, ch)[:sp_rows].astype(F32).reshape(3, 3, ch, ch)]
where the time goes in v3:
time: 99.2 us; the launch traced here: 99.1 us
  Pallas kernels  98.4 us (99%)
    pallas_call x1, Pallas kernels, local(): pl.pallas_call(functools.partial(kernel, n), out_shape=(jax.ShapeDtypeStr...  51.6 us
    pallas_call x1, Pallas kernels, hand_over(): pl.pallas_call(body, out_shape=tuple((jax.ShapeDtypeStruct(a.shape, a.dty...  46.8 us

profile of v3, /device:TPU:1, one launch (start us, length us, event | category | flops | bytes accessed | tf_op | source)
XLA Modules:
  0.0 99.1 jit_solution(13499462836137155451)
XLA Ops:
  0.6 51.6 %shard_map.85 = (bf16[32,64,128]{2,1,0:T(8,128)(2,1)}, f32[1152,128]{1,0:T(8,128)}, f32[768,128]{1,0:T(8,128)}) custom-call(s32[2]{0:T(128)} %dil_ref.1, s32[2,3]{1,0:T(2,128)} %off_ref.1, bf16[2,32,128,128]{3,2,1,0:T(8,128)(2,1)} %frames_hbm.1, bf16[1152,128]{1,0:T(8,128)(2,1)} %bitcast.6, bf16[2,384,128]{2,1,0:T(8,128)(2,1)} %bitcast.7, ...), custom_call_target="tpu_custom_call" | custom-call | flops 2415919104 | bytes 8388608 | tf_op jit(solution)/shard_map/pallas_call | solution.py:453
  52.3 46.8 %shard_map.86 = (bf16[32,64,128]{2,1,0:T(8,128)(2,1)}, f32[1152,128]{1,0:T(8,128)}, f32[768,128]{1,0:T(8,128)}) custom-call(bf16[32,64,128]{2,1,0:T(8,128)(2,1)} %get-tuple-element.9.refs_0_, f32[1152,128]{1,0:T(8,128)} %get-tuple-element.10.refs_1_, f32[768,128]{1,0:T(8,128)} %get-tuple-element.11.refs_2_), custom_call_target="tpu_custom_call" | custom-call | tf_op jit(solution)/shard_map/pallas_call | solution.py:430

commit v4 on v3

--- a/solution.py
+++ b/solution.py
@@ -11,6 +11,8 @@
 F32 = jnp.float32
 MESH = pl.DeviceIdType.MESH
 PARTS = 4
+NEAR_S = 2
+NEAR_T = 4
 
 
 def remote(src, dst, send, recv, to):
@@ -29,84 +31,84 @@
 
 
 class Reduce:
-    def __init__(self, n, out, total, pair_out, pair_in, chip_out, chip_in, own, gathered, send, recv):
-        self.total, self.pair_out, self.pair_in = total, pair_out, pair_in
-        self.chip_out, self.chip_in, self.own = chip_out, chip_in, own
-        self.gathered, self.send, self.recv, self.out = gathered, send, recv, out
-        self.chips = n // 2
+    def __init__(self, n, size, out, total, near_out, near_in, far_out, far_in, own, gathered, *sems):
+        self.out, self.total, self.near_out, self.near_in = out, total, near_out, near_in
+        self.far_out, self.far_in, self.own, self.gathered = far_out, far_in, own, gathered
+        self.send, self.recv = sems
+        self.size, self.groups = size, n // size
         me = lax.axis_index("seq")
-        self.core, self.chip = lax.rem(me, 2), me // 2
-        self.partner = me + 1 - 2 * self.core
+        self.near, self.far = lax.rem(me, size), me // size
         self.rows, self.ch = own.shape
-        self.half = self.chips * self.rows
-        self.pair = remote(
-            pair_out.at[1 - self.core], pair_in, send.at[0], recv.at[0], self.partner
-        )
-        self.swap = remote(
-            gathered.at[self.core], gathered.at[self.core], send.at[3], recv.at[3], self.partner
-        )
+        self.slab = self.groups * self.rows
+
+    def near_loop(self, src_of, dst, hop):
+        for k in range(1, self.size):
+            c = lax.rem(self.near + k, self.size)
+            to = self.far * self.size + c
+            remote(src_of(c), dst, self.send.at[hop], self.recv.at[hop], to).start()
+
+    def far_loop(self, src_of, dst, hop):
+        def step(k, carry):
+            g = lax.rem(self.far + k, self.groups)
+            to = g * self.size + self.near
+            remote(src_of(g), dst, self.send.at[hop], self.recv.at[hop], to).start()
+            return carry
+
+        lax.fori_loop(1, self.groups, step, 0)
+
+    def span(self, c):
+        return pl.ds(pl.multiple_of(c * self.slab, self.slab), self.slab)
 
     def pieces(self, x):
-        return x.reshape(self.chips, self.rows, self.ch)
-
-    def chips_loop(self, src_of, dst, hop):
-        def step(k, carry):
-            c = lax.rem(self.chip + k, self.chips)
-            remote(
-                src_of(c), dst, self.send.at[hop], self.recv.at[hop], 2 * c + self.core
-            ).start()
-            return carry
-
-        lax.fori_loop(1, self.chips, step, 0)
+        return x.reshape(self.groups, self.rows, self.ch)
 
     def start(self):
-        for c in range(2):
-            part = self.total[c * self.half : (c + 1) * self.half, :]
-            self.pair_out[c] = self.pieces(part.astype(BF16))
-        self.pair.start()
+        for c in range(self.size):
+            part = self.total[c * self.slab : (c + 1) * self.slab, :]
+            self.near_out[c] = self.pieces(part.astype(BF16))
+        self.near_loop(lambda c: self.near_out.at[c], self.near_in.at[self.near], 0)
 
     def scatter(self):
-        at = pl.multiple_of(self.core * self.half, self.half)
-        mine = self.pieces(self.total[pl.ds(at, self.half), :])
-        self.pair.wait_recv()
-        self.chip_out[...] = (mine + self.pair_in[...].astype(F32)).astype(BF16)
-        dst = self.chip_in.at[self.chip]
-        self.chips_loop(lambda c: self.chip_out.at[c], dst, 1)
-        pltpu.make_async_copy(self.chip_out.at[self.chip], dst, self.recv.at[1]).start()
+        mine = self.pieces(self.total[self.span(self.near), :])
+        drain(self.near_in.at[pl.ds(0, self.size - 1)], self.recv.at[0])
+        for k in range(1, self.size):
+            mine = mine + self.near_in[lax.rem(self.near + k, self.size)].astype(F32)
+        self.far_out[...] = mine.astype(BF16)
+        dst = self.far_in.at[self.far]
+        self.far_loop(lambda g: self.far_out.at[g], dst, 1)
+        pltpu.make_async_copy(self.far_out.at[self.far], dst, self.recv.at[1]).start()
 
     def gather(self):
-        drain(self.chip_in, self.recv.at[1])
-        self.own[...] = jnp.sum(self.chip_in[...].astype(F32), axis=0).astype(BF16)
-        dst = self.gathered.at[self.core, self.chip]
-        self.chips_loop(lambda c: self.own, dst, 2)
+        drain(self.far_in, self.recv.at[1])
+        self.own[...] = jnp.sum(self.far_in[...].astype(F32), axis=0).astype(BF16)
+        dst = self.gathered.at[self.near, self.far]
+        self.far_loop(lambda g: self.own, dst, 2)
         pltpu.make_async_copy(self.own, dst, self.recv.at[2]).start()
 
     def exchange(self):
-        drain(self.gathered.at[self.core], self.recv.at[2])
-        self.swap.start()
-        self.widen(self.core)
+        mine = self.gathered.at[self.near]
+        drain(mine, self.recv.at[2])
+        self.near_loop(lambda c: mine, mine, 3)
+        self.widen(self.near)
 
     def finish(self):
-        self.swap.wait_recv()
-        self.widen(1 - self.core)
+        drain(self.near_in.at[pl.ds(0, self.size - 1)], self.recv.at[3])
+        for k in range(1, self.size):
+            self.widen(lax.rem(self.near + k, self.size))
         self.store().start()
 
-    def widen(self, side):
-        at = pl.multiple_of(side * self.half, self.half)
-        self.total[pl.ds(at, self.half), :] = (
-            self.gathered[side].astype(F32).reshape(self.half, self.ch)
-        )
+    def widen(self, c):
+        self.total[self.span(c), :] = self.gathered[c].astype(F32).reshape(self.slab, self.ch)
 
     def store(self):
         held = self.total.at[pl.ds(0, self.out.shape[0])]
         return pltpu.make_async_copy(held, self.out, self.recv.at[4])
 
     def sent(self):
-        self.pair.wait_send()
-        self.swap.wait_send()
-        most = self.chip_out.at[pl.ds(0, self.chips - 1)]
-        drain(most, self.send.at[1])
-        drain(most, self.send.at[2])
+        for hop in (0, 3):
+            drain(self.near_in.at[pl.ds(0, self.size - 1)], self.send.at[hop])
+        for hop in (1, 2):
+            drain(self.far_out.at[pl.ds(0, self.groups - 1)], self.send.at[hop])
         self.store().wait()
 
 
@@ -144,11 +146,11 @@
     turned_t,
     *rest,
 ):
-    red_s = Reduce(n, gs_hbm, sum_s, *rest[0:8])
-    red_t = Reduce(n, gt_hbm, sum_t, *rest[8:16])
+    red_s = Reduce(n, NEAR_S, gs_hbm, sum_s, *rest[0:8])
+    red_t = Reduce(n, NEAR_T, gt_hbm, sum_t, *rest[8:16])
     send1, recv1, send2, recv2, load = rest[16:]
     me = lax.axis_index("seq")
-    per, height, width, ch = frames_ref.shape
+    per, height, width, ch = frames_hbm.shape
     length, pix, _ = cot_ref.shape
     layers, taps = off_ref.shape
     parts, _, _, pp, _ = spat.shape
@@ -164,11 +166,23 @@
     sp_rows = ws_ref.shape[0]
     tap_rows = taps * ch
 
+    my_q = me // q_devs
+    q_in = height // q_count
+
+    for s in range(q_count):
+        q = lax.rem(my_q + 1 + s, q_count)
+        above = jnp.maximum(q * q_in - 1, 0)
+        for f in range(per):
+            pltpu.make_async_copy(
+                frames_hbm.at[f, pl.ds(q * q_in, q_in)],
+                frames_ref.at[q, f, pl.ds(1, q_in)],
+                load.at[q],
+            ).start()
+            pltpu.make_async_copy(
+                frames_hbm.at[f, pl.ds(above, 1)], frames_ref.at[q, f, pl.ds(0, 1)], load.at[q]
+            ).start()
     fetch = [
-        pltpu.make_async_copy(frames_hbm.at[f], frames_ref.at[f], load.at[f]) for f in range(per)
-    ]
-    fetch += [
-        pltpu.make_async_copy(a, b, load.at[per + i])
+        pltpu.make_async_copy(a, b, load.at[q_count + i])
         for i, (a, b) in enumerate([(ws_hbm, ws_ref), (wt_hbm, wt_ref), (cot_hbm, cot_ref)])
     ]
     for copy in fetch:
@@ -195,28 +209,24 @@
 
     lax.fori_loop(1, n, greet, 0)
 
-    group = tmp.shape[0]
-    for g in range(group):
-        tmp[g, 0:8, :] = jnp.zeros((8, ch), F32)
     for f in range(per):
-        xcols[f, 0, 0] = jnp.zeros((parts, cw, 3 * ch), BF16)
-
-    for f in range(per):
-        fetch[f].wait()
-
-        def spread(step, carry):
-            for g in range(group):
-                tmp[g, 8 : 8 + width, :] = frames_ref[f, step * group + g].astype(F32)
-            for g in range(group):
-                row = step * (group // 2) + (g + 1) // 2
+        for g in range(q_in + 1):
+            tmp[f, g, 0:8, :] = jnp.zeros((8, ch), F32)
+
+    def spread(q):
+        drain(frames_ref.at[q], load.at[q])
+        for f in range(per):
+            for g in range(q_in + 1):
+                row = frames_ref[q, f, g].astype(F32)
+                if g == 0:
+                    row = jnp.where(q > 0, row, 0.0)
+                tmp[f, g, 8 : 8 + width, :] = row
+            for g in range(q_in + 1):
                 for b in range(3):
-                    col = tmp[g, pl.ds(7 + b, out_w, stride=2), :].astype(BF16)
-                    xcols[f, row, (g + 1) % 2, :, :, b * ch : (b + 1) * ch] = col.reshape(
-                        parts, cw, ch
+                    col = tmp[f, g, pl.ds(7 + b, out_w, stride=2), :].astype(BF16)
+                    xcols[f, q * q_rows + g // 2, g % 2, :, :, b * ch : (b + 1) * ch] = (
+                        col.reshape(parts, cw, ch)
                     )
-            return carry
-
-        lax.fori_loop(0, height // group, spread, 0)
 
     def row_taps(f, i0, count, *part):
         views = [
@@ -226,10 +236,7 @@
         ]
         return jnp.concatenate([v.reshape(-1, 3 * ch) for v in views], axis=1)
 
-    fetch[per].wait()
-    pl.semaphore_wait(barrier, n - 1)
-
-    my_q = me // q_devs
+    early = max(1, parts // 2)
     mine = pl.ds(me * per, per)
 
     def send_map(h, j):
@@ -244,6 +251,12 @@
     def conv(s, carry):
         q = lax.rem(my_q + 1 + s, q_count)
         devs = pl.ds(q * q_devs, q_devs)
+        spread(q)
+
+        @pl.when(s == 0)
+        def _():
+            fetch[0].wait()
+
         x = jnp.concatenate([row_taps(f, q * q_rows, q_rows) for f in range(per)], axis=0)
         out = jnp.dot(x, ws_ref[...], preferred_element_type=F32)
         out = out.reshape(per, q_devs, parts, pp, ch).astype(BF16)
@@ -251,8 +264,13 @@
             for h in range(parts):
                 spat[h, devs, f] = out[f, :, h]
 
+        @pl.when(s == 0)
+        def _():
+            pl.semaphore_wait(barrier, n - 1)
+
         def first(k, c):
-            send_map(0, q * q_devs + lax.rem(me + k, q_devs))
+            for h in range(early):
+                send_map(h, q * q_devs + lax.rem(me + k, q_devs))
             return c
 
         lax.fori_loop(0, q_devs, first, 0)
@@ -261,13 +279,13 @@
     lax.fori_loop(0, q_count, conv, 0)
 
     def later(i, carry):
-        send_map(1 + i // n, lax.rem(me + 1 + lax.rem(i, n), n))
+        send_map(early + i // n, lax.rem(me + 1 + lax.rem(i, n), n))
         return carry
 
-    lax.fori_loop(0, (parts - 1) * n, later, 0)
-
-    fetch[per + 1].wait()
-    fetch[per + 2].wait()
+    lax.fori_loop(0, (parts - early) * n, later, 0)
+
+    fetch[1].wait()
+    fetch[2].wait()
 
     def clear(t, carry):
         zero = jnp.zeros((t_len, pp, ch), BF16)
@@ -397,44 +415,20 @@
             drain(spat.at[h, pl.ds(0, n - 1)], sem)
 
 
-def reduce_scratch(n, total_rows, ch):
-    chips = n // 2
+def reduce_scratch(n, size, total_rows, ch):
+    groups = n // size
     rows = -(-total_rows // (16 * n)) * 16
     dma = pltpu.SemaphoreType.DMA
     return rows * n, [
-        pltpu.VMEM((2, chips, rows, ch), BF16),
-        pltpu.VMEM((chips, rows, ch), BF16),
-        pltpu.VMEM((chips, rows, ch), BF16),
-        pltpu.VMEM((chips, rows, ch), BF16),
+        pltpu.VMEM((size, groups, rows, ch), BF16),
+        pltpu.VMEM((size, groups, rows, ch), BF16),
+        pltpu.VMEM((groups, rows, ch), BF16),
+        pltpu.VMEM((groups, rows, ch), BF16),
         pltpu.VMEM((rows, ch), BF16),
-        pltpu.VMEM((2, chips, rows, ch), BF16),
+        pltpu.VMEM((size, groups, rows, ch), BF16),
         dma((4,)),
         dma((5,)),
     ]
-
-
-def hand_over(*arrays):
-    count = len(arrays)
-
-    def body(*refs):
-        sems = refs[2 * count]
-        copies = [
-            pltpu.make_async_copy(refs[i], refs[count + i], sems.at[i]) for i in range(count)
-        ]
-        for copy in copies:
-            copy.start()
-        for copy in copies:
-            copy.wait()
-
-    hbm = pl.BlockSpec(memory_space=pltpu.HBM)
-    return pl.pallas_call(
-        body,
-        out_shape=tuple(jax.ShapeDtypeStruct(a.shape, a.dtype) for a in arrays),
-        in_specs=[hbm] * count,
-        out_specs=(hbm,) * count,
-        scratch_shapes=[pltpu.SemaphoreType.DMA((count,))],
-        compiler_params=pltpu.CompilerParams(vmem_limit_bytes=60 * 1024 * 1024),
-    )(*arrays)
 
 
 def local(n, frames, w_spatial, w_temporal, dilations, offsets, cotangent):
@@ -445,8 +439,8 @@
     sp_rows, tp_rows = 9 * ch, layers * taps * ch
     parts = PARTS if pix == out_w and pix % (16 * PARTS) == 0 else 1
     pp = pix // parts
-    pad_s, red_s = reduce_scratch(n, sp_rows, ch)
-    pad_t, red_t = reduce_scratch(n, tp_rows, ch)
+    pad_s, red_s = reduce_scratch(n, NEAR_S, sp_rows, ch)
+    pad_t, red_t = reduce_scratch(n, NEAR_T, tp_rows, ch)
     smem = pl.BlockSpec(memory_space=pltpu.SMEM)
     hbm = pl.BlockSpec(memory_space=pltpu.HBM)
     dma = pltpu.SemaphoreType.DMA
@@ -461,11 +455,11 @@
         out_specs=(hbm, hbm, hbm),
         scratch_shapes=[
             pltpu.VMEM(cotangent.shape, BF16),
-            pltpu.VMEM(frames.shape, BF16),
+            pltpu.VMEM((4, per, height // 4 + 1, width, ch), BF16),
             pltpu.VMEM((sp_rows, ch), BF16),
             pltpu.VMEM((layers, taps * ch, ch), BF16),
             pltpu.VMEM(cotangent.shape, BF16),
-            pltpu.VMEM((8, width + 8, ch), F32),
+            pltpu.VMEM((per, height // 4 + 1, width + 8, ch), F32),
             pltpu.VMEM((per, out_h + 1, 2, parts, out_w // parts, 3 * ch), BF16),
             pltpu.VMEM((parts, n, per, pp, ch), BF16),
             pltpu.VMEM((parts, length, pp, ch), BF16),
@@ -487,7 +481,7 @@
             dma((parts,)),
             dma,
             dma((parts,)),
-            dma((per + 3,)),
+            dma((4 + 3,)),
         ],
         compiler_params=pltpu.CompilerParams(
             collective_id=0, has_side_effects=True, vmem_limit_bytes=60 * 1024 * 1024
@@ -503,7 +497,6 @@
         w_temporal.reshape(layers, taps * ch, ch),
         cotangent,
     )
-    features, grad_spatial, grad_temporal = hand_over(features, grad_spatial, grad_temporal)
     return (
         features,
         grad_spatial.reshape(3, 3, ch, ch),

time: 99.2 us -> 56.6 us (0.57)
  Pallas kernels: 98.4 us -> 51.1 us
  local copies, waits for them, and re-layouts: 0 us -> 4.58 us
    pallas_call x1 -> x0, Pallas kernels: 46.8 us -> none  [hand_over(): pl.pallas_call(body, out_shape=tuple((jax.ShapeDtypeStruct(a.shape, a.dty...]
    unnamed x0 -> x5, local copies, waits for them, and re-layouts: none -> 4.58 us
where the time goes in v4:
time: 56.6 us; the launch traced here: 56.3 us
  Pallas kernels  51.1 us (90%)
  local copies, waits for them, and re-layouts  4.58 us (8%)
  between operations  0.65 us (1%)
    pallas_call x1, Pallas kernels, local(): pl.pallas_call(functools.partial(kernel, n), out_shape=(jax.ShapeDtypeStr...  51.1 us
    unnamed x5, local copies, waits for them, and re-layouts  4.58 us

profile of v4, /device:TPU:1, one launch (start us, length us, event | category | flops | bytes accessed | tf_op | source)
XLA Modules:
  0.0 56.3 jit_solution(9319850958977573646)
XLA Ops:
  0.6 51.1 %shard_map.85 = (bf16[32,64,128]{2,1,0:T(8,128)(2,1)}, f32[1152,128]{1,0:T(8,128)}, f32[768,128]{1,0:T(8,128)}) custom-call(s32[2]{0:T(128)} %dil_ref.1, s32[2,3]{1,0:T(2,128)} %off_ref.1, bf16[2,32,128,128]{3,2,1,0:T(8,128)(2,1)} %frames_hbm.1, bf16[1152,128]{1,0:T(8,128)(2,1)} %bitcast.6, bf16[2,384,128]{2,1,0:T(8,128)(2,1)} %bitcast.7, ...), custom_call_target="tpu_custom_call" | custom-call | flops 2415919104 | bytes 8388608 | tf_op jit(solution)/shard_map/pallas_call | solution.py:447
  51.7 0.0 copy-start
  51.7 1.9 %copy.12 = bf16[32,64,128]{2,1,0:T(8,128)(2,1)} copy(bf16[32,64,128]{2,1,0:T(8,128)(2,1)} %get-tuple-element.12) | data formatting | bytes 1048576
  53.7 1.9 %copy.13 = f32[3,3,128,128]{3,2,1,0:T(8,128)} copy(f32[3,3,128,128]{3,2,1,0:T(8,128)} %bitcast.4) | data formatting | bytes 1179648
  55.6 0.0 copy-done
  55.6 0.7 %copy.14 = f32[2,3,128,128]{3,2,1,0:T(8,128)} copy(f32[2,3,128,128]{3,2,1,0:T(8,128)S(1)} %bitcast.5) | data formatting | bytes 786432
Async XLA Ops:
  51.7 3.8 %copy-start = (f32[768,128]{1,0:T(8,128)S(1)}, f32[768,128]{1,0:T(8,128)}, u32[]{:S(2)}) copy-start(f32[768,128]{1,0:T(8,128)} %get-tuple-element.8) | copy-start | bytes 1179652

commit v5 on v4

--- a/solution.py
+++ b/solution.py
@@ -10,9 +10,21 @@
 BF16 = jnp.bfloat16
 F32 = jnp.float32
 MESH = pl.DeviceIdType.MESH
-PARTS = 4
+PARTS = 2
 NEAR_S = 2
 NEAR_T = 4
+
+
+def wrap(x, n):
+    return jnp.where(x >= n, x - n, x)
+
+
+def each(first, end, body):
+    if end - first <= 16:
+        for k in range(first, end):
+            body(k)
+    else:
+        lax.fori_loop(first, end, lambda k, c: (body(k), c)[1], 0)
 
 
 def remote(src, dst, send, recv, to):
@@ -43,18 +55,17 @@
 
     def near_loop(self, src_of, dst, hop):
         for k in range(1, self.size):
-            c = lax.rem(self.near + k, self.size)
+            c = wrap(self.near + k, self.size)
             to = self.far * self.size + c
             remote(src_of(c), dst, self.send.at[hop], self.recv.at[hop], to).start()
 
     def far_loop(self, src_of, dst, hop):
-        def step(k, carry):
-            g = lax.rem(self.far + k, self.groups)
+        def step(k):
+            g = wrap(self.far + k, self.groups)
             to = g * self.size + self.near
             remote(src_of(g), dst, self.send.at[hop], self.recv.at[hop], to).start()
-            return carry
-
-        lax.fori_loop(1, self.groups, step, 0)
+
+        each(1, self.groups, step)
 
     def span(self, c):
         return pl.ds(pl.multiple_of(c * self.slab, self.slab), self.slab)
@@ -72,7 +83,7 @@
         mine = self.pieces(self.total[self.span(self.near), :])
         drain(self.near_in.at[pl.ds(0, self.size - 1)], self.recv.at[0])
         for k in range(1, self.size):
-            mine = mine + self.near_in[lax.rem(self.near + k, self.size)].astype(F32)
+            mine = mine + self.near_in[wrap(self.near + k, self.size)].astype(F32)
         self.far_out[...] = mine.astype(BF16)
         dst = self.far_in.at[self.far]
         self.far_loop(lambda g: self.far_out.at[g], dst, 1)
@@ -89,27 +100,22 @@
         mine = self.gathered.at[self.near]
         drain(mine, self.recv.at[2])
         self.near_loop(lambda c: mine, mine, 3)
-        self.widen(self.near)
+        self.store(self.near)
 
     def finish(self):
         drain(self.near_in.at[pl.ds(0, self.size - 1)], self.recv.at[3])
         for k in range(1, self.size):
-            self.widen(lax.rem(self.near + k, self.size))
-        self.store().start()
-
-    def widen(self, c):
-        self.total[self.span(c), :] = self.gathered[c].astype(F32).reshape(self.slab, self.ch)
-
-    def store(self):
-        held = self.total.at[pl.ds(0, self.out.shape[0])]
-        return pltpu.make_async_copy(held, self.out, self.recv.at[4])
+            self.store(wrap(self.near + k, self.size))
+
+    def store(self, c):
+        pltpu.make_async_copy(self.gathered.at[c], self.out.at[c], self.recv.at[4]).start()
 
     def sent(self):
         for hop in (0, 3):
             drain(self.near_in.at[pl.ds(0, self.size - 1)], self.send.at[hop])
         for hop in (1, 2):
             drain(self.far_out.at[pl.ds(0, self.groups - 1)], self.send.at[hop])
-        self.store().wait()
+        drain(self.gathered, self.recv.at[4])
 
 
 def kernel(
@@ -201,13 +207,12 @@
 
     barrier = pltpu.get_barrier_semaphore()
 
-    def greet(s, carry):
+    def greet(s):
         pl.semaphore_signal(
-            barrier, inc=1, device_id={"seq": lax.rem(me + s, n)}, device_id_type=MESH
+            barrier, inc=1, device_id={"seq": wrap(me + s, n)}, device_id_type=MESH
         )
-        return carry
-
-    lax.fori_loop(1, n, greet, 0)
+
+    each(1, n, greet)
 
     for f in range(per):
         for g in range(q_in + 1):
@@ -240,13 +245,7 @@
     mine = pl.ds(me * per, per)
 
     def send_map(h, j):
-        @pl.when(j != me)
-        def _():
-            remote(spat.at[h, j], land.at[h, mine], send1, recv1.at[h], j).start()
-
-        @pl.when(j == me)
-        def _():
-            pltpu.make_async_copy(spat.at[h, j], land.at[h, mine], recv1.at[h]).start()
+        remote(spat.at[h, j], land.at[h, mine], send1, recv1.at[h], j).start()
 
     def conv(s, carry):
         q = lax.rem(my_q + 1 + s, q_count)
@@ -268,21 +267,32 @@
         def _():
             pl.semaphore_wait(barrier, n - 1)
 
-        def first(k, c):
-            for h in range(early):
-                send_map(h, q * q_devs + lax.rem(me + k, q_devs))
-            return c
-
-        lax.fori_loop(0, q_devs, first, 0)
+        @pl.when(s < q_count - 1)
+        def _():
+            def first(k):
+                j = q * q_devs + wrap(me - my_q * q_devs + k, q_devs)
+                for h in range(early):
+                    send_map(h, j)
+
+            each(0, q_devs, first)
+
+        @pl.when(s == q_count - 1)
+        def _():
+            def last(k):
+                j = q * q_devs + wrap(me - my_q * q_devs + k, q_devs)
+                for h in range(early):
+                    send_map(h, j)
+
+            each(1, q_devs, last)
+
         return carry
 
     lax.fori_loop(0, q_count, conv, 0)
 
-    def later(i, carry):
-        send_map(early + i // n, lax.rem(me + 1 + lax.rem(i, n), n))
-        return carry
-
-    lax.fori_loop(0, (parts - early) * n, later, 0)
+    for h in range(early, parts):
+        each(1, n, lambda k: send_map(h, wrap(me + k, n)))
+    for h in range(parts):
+        pltpu.make_async_copy(spat.at[h, me], land.at[h, mine], recv1.at[h]).start()
 
     fetch[1].wait()
     fetch[2].wait()
@@ -360,14 +370,13 @@
 
         steps(t_count, backward)
 
-        def send(k, c):
-            j = lax.rem(me + k, n)
+        def send(k):
+            j = wrap(me + k, n)
             remote(
                 maps.at[h, pl.ds(j * per, per)], back.at[h, me], send2, recv2.at[h], j
             ).start()
-            return c
-
-        lax.fori_loop(1, n, send, 0)
+
+        each(1, n, send)
         pltpu.make_async_copy(maps.at[h, mine], back.at[h, me], recv2.at[h]).start()
         return carry
 
@@ -390,20 +399,19 @@
         for k in range(taps):
             at = layer * tap_rows + k * ch
             sum_t[at : at + ch, :] = turned_t[layer, :, k * ch : (k + 1) * ch].T
-    hops = [red_t.start, red_t.scatter, red_t.gather, red_t.exchange]
-    hops[0]()
+    red_t.start()
     for h in range(parts):
         conv_grad(h)
-        if h + 1 < min(parts, len(hops)):
-            hops[h + 1]()
+        if h == 0:
+            red_t.scatter()
     for at in range(0, sp_rows, ch):
         sum_s[at : at + ch, :] = turned_s[:, at : at + ch].T
     red_s.start()
-    for hop in hops[max(1, min(parts, len(hops))) :]:
-        hop()
+    red_t.gather()
     red_s.scatter()
+    red_t.exchange()
+    red_s.gather()
     red_t.finish()
-    red_s.gather()
     red_s.exchange()
     red_s.finish()
 
@@ -429,6 +437,53 @@
         dma((4,)),
         dma((5,)),
     ]
+
+
+def widen(features, spatial, temporal, sp_rows, tp_rows):
+    ch = spatial.shape[1]
+
+    def body(feat_in, s_in, t_in, feat_out, s_out, t_out, feat, s, t, s32, t32, sems):
+        loads = [
+            pltpu.make_async_copy(src, dst, sems.at[i])
+            for i, (src, dst) in enumerate([(feat_in, feat), (s_in, s), (t_in, t)])
+        ]
+        stores = [
+            pltpu.make_async_copy(src, dst, sems.at[3 + i])
+            for i, (src, dst) in enumerate([(feat, feat_out), (s32, s_out), (t32, t_out)])
+        ]
+        for copy in loads:
+            copy.start()
+        loads[0].wait()
+        stores[0].start()
+        loads[1].wait()
+        s32[...] = s[:sp_rows].astype(F32)
+        stores[1].start()
+        loads[2].wait()
+        t32[...] = t[:tp_rows].astype(F32)
+        stores[2].start()
+        for copy in stores:
+            copy.wait()
+
+    hbm = pl.BlockSpec(memory_space=pltpu.HBM)
+    return pl.pallas_call(
+        body,
+        out_shape=(
+            jax.ShapeDtypeStruct(features.shape, BF16),
+            jax.ShapeDtypeStruct((sp_rows, ch), F32),
+            jax.ShapeDtypeStruct((tp_rows, ch), F32),
+        ),
+        in_specs=[hbm] * 3,
+        out_specs=(hbm,) * 3,
+        scratch_shapes=[
+            pltpu.VMEM(features.shape, BF16),
+            pltpu.VMEM(spatial.shape, BF16),
+            pltpu.VMEM(temporal.shape, BF16),
+            pltpu.VMEM((sp_rows, ch), F32),
+            pltpu.VMEM((tp_rows, ch), F32),
+            pltpu.SemaphoreType.DMA((6,)),
+        ],
+        compiler_params=pltpu.CompilerParams(vmem_limit_bytes=60 * 1024 * 1024),
+    )(features, spatial, temporal)
 
 
 def local(n, frames, w_spatial, w_temporal, dilations, offsets, cotangent):
@@ -448,8 +503,8 @@
         functools.partial(kernel, n),
         out_shape=(
             jax.ShapeDtypeStruct((length, pix, ch), BF16),
-            jax.ShapeDtypeStruct((sp_rows, ch), F32),
-            jax.ShapeDtypeStruct((tp_rows, ch), F32),
+            jax.ShapeDtypeStruct((NEAR_S, n // NEAR_S, pad_s // n, ch), BF16),
+            jax.ShapeDtypeStruct((NEAR_T, n // NEAR_T, pad_t // n, ch), BF16),
         ),
         in_specs=[smem, smem, hbm, hbm, hbm, hbm],
         out_specs=(hbm, hbm, hbm),
@@ -497,6 +552,9 @@
         w_temporal.reshape(layers, taps * ch, ch),
         cotangent,
     )
+    features, grad_spatial, grad_temporal = widen(
+        features, grad_spatial.reshape(-1, ch), grad_temporal.reshape(-1, ch), sp_rows, tp_rows
+    )
     return (
         features,
         grad_spatial.reshape(3, 3, ch, ch),

time: 56.6 us -> 49.9 us (0.88)
  local copies, waits for them, and re-layouts: 4.58 us -> 0 us
  Pallas kernels: 51.1 us -> 49.1 us
    unnamed x5 -> x0, local copies, waits for them, and re-layouts: 4.58 us -> none
    pallas_call x1, Pallas kernels: 51.1 us -> 46.9 us  [local(): pl.pallas_call(functools.partial(kernel, n), out_shape=(jax.ShapeDtypeStr...]
    pallas_call x0 -> x1, Pallas kernels: none -> 2.21 us  [widen(): pl.pallas_call(body, out_shape=(jax.ShapeDtypeStruct(features.shape, BF16...]
where the time goes in v5:
time: 49.9 us; the launch traced here: 49.8 us
  Pallas kernels  49.1 us (98%)
  between operations  0.64 us (1%)
    pallas_call x1, Pallas kernels, local(): pl.pallas_call(functools.partial(kernel, n), out_shape=(jax.ShapeDtypeStr...  46.9 us
    pallas_call x1, Pallas kernels, widen(): pl.pallas_call(body, out_shape=(jax.ShapeDtypeStruct(features.shape, BF16...  2.21 us

profile of v5, /device:TPU:1, one launch (start us, length us, event | category | flops | bytes accessed | tf_op | source)
XLA Modules:
  0.0 49.8 jit_solution(12021296528005584844)
XLA Ops:
  0.6 46.9 %shard_map.85 = (bf16[32,64,128]{2,1,0:T(8,128)(2,1)}, bf16[2,8,80,128]{3,2,1,0:T(8,128)(2,1)}, bf16[4,4,48,128]{3,2,1,0:T(8,128)(2,1)}) custom-call(s32[2]{0:T(128)} %dil_ref.1, s32[2,3]{1,0:T(2,128)} %off_ref.1, bf16[2,32,128,128]{3,2,1,0:T(8,128)(2,1)} %frames_hbm.1, bf16[1152,128]{1,0:T(8,128)(2,1)} %bitcast.10, bf16[2,384,128]{2,1,0:T(8,128)(2,1)} %bitcast.11, ...), custom_call_target="tpu_custom_call" | custom-call | flops 2415919104 | bytes 8388608 | tf_op jit(solution)/shard_map/pallas_call | solution.py:502
  47.5 2.2 %shard_map.86 = (bf16[32,64,128]{2,1,0:T(8,128)(2,1)}, f32[1152,128]{1,0:T(8,128)}, f32[768,128]{1,0:T(8,128)}) custom-call(bf16[32,64,128]{2,1,0:T(8,128)(2,1)} %get-tuple-element.9.feat_in, bf16[1280,128]{1,0:T(8,128)(2,1)} %bitcast.6, bf16[768,128]{1,0:T(8,128)(2,1)} %bitcast.7), custom_call_target="tpu_custom_call" | custom-call | tf_op jit(solution)/shard_map/pallas_call | solution.py:468

commit v6 on v5

--- a/solution.py
+++ b/solution.py
@@ -25,6 +25,15 @@
             body(k)
     else:
         lax.fori_loop(first, end, lambda k, c: (body(k), c)[1], 0)
+
+
+def others(n, body):
+    half = n // 2
+    if n <= 16:
+        for k in sorted(range(1, n), key=lambda k: abs(k - half)):
+            body(k)
+    else:
+        lax.fori_loop(0, n - 1, lambda k, c: (body(1 + lax.rem(half - 1 + k, n - 1)), c)[1], 0)
 
 
 def remote(src, dst, send, recv, to):
@@ -65,7 +74,7 @@
             to = g * self.size + self.near
             remote(src_of(g), dst, self.send.at[hop], self.recv.at[hop], to).start()
 
-        each(1, self.groups, step)
+        others(self.groups, step)
 
     def span(self, c):
         return pl.ds(pl.multiple_of(c * self.slab, self.slab), self.slab)
@@ -165,8 +174,6 @@
     q_count = 4
     q_rows = out_h // q_count
     q_devs = n // q_count
-    g_count = max(1, per * out_h * cw // 512)
-    g_rows, g_devs = out_h // g_count, n // g_count
     t_count = max(1, length * pp // 512)
     t_len = length // t_count
     sp_rows = ws_ref.shape[0]
@@ -175,8 +182,12 @@
     my_q = me // q_devs
     q_in = height // q_count
 
+    def quarter(s):
+        step = jnp.where(s == 0, 2, jnp.where(s == 1, 1, jnp.where(s == 2, 3, 0)))
+        return wrap(my_q + step, q_count)
+
     for s in range(q_count):
-        q = lax.rem(my_q + 1 + s, q_count)
+        q = quarter(s)
         above = jnp.maximum(q * q_in - 1, 0)
         for f in range(per):
             pltpu.make_async_copy(
@@ -248,7 +259,7 @@
         remote(spat.at[h, j], land.at[h, mine], send1, recv1.at[h], j).start()
 
     def conv(s, carry):
-        q = lax.rem(my_q + 1 + s, q_count)
+        q = quarter(s)
         devs = pl.ds(q * q_devs, q_devs)
         spread(q)
 
@@ -290,7 +301,7 @@
     lax.fori_loop(0, q_count, conv, 0)
 
     for h in range(early, parts):
-        each(1, n, lambda k: send_map(h, wrap(me + k, n)))
+        others(n, lambda k: send_map(h, wrap(me + k, n)))
     for h in range(parts):
         pltpu.make_async_copy(spat.at[h, me], land.at[h, mine], recv1.at[h]).start()
 
@@ -373,25 +384,25 @@
         def send(k):
             j = wrap(me + k, n)
             remote(
-                maps.at[h, pl.ds(j * per, per)], back.at[h, me], send2, recv2.at[h], j
+                maps.at[h, pl.ds(j * per, per)], back.at[h, me], send2, recv2.at[h, my_q], j
             ).start()
 
-        each(1, n, send)
-        pltpu.make_async_copy(maps.at[h, mine], back.at[h, me], recv2.at[h]).start()
+        others(n, send)
+        pltpu.make_async_copy(maps.at[h, mine], back.at[h, me], recv2.at[h, my_q]).start()
         return carry
 
     lax.fori_loop(0, parts, temporal, 0)
 
     def conv_grad(h):
-        drain(back.at[h], recv2.at[h])
-
-        def rows(s):
-            i0 = s * g_rows
-            x = jnp.concatenate([row_taps(f, i0, g_rows, h) for f in range(per)], axis=0)
-            g = [flat(back[h, pl.ds(s * g_devs, g_devs), f]) for f in range(per)]
-            turned_s[...] += outer(jnp.concatenate(g, axis=0), x)
-
-        steps(g_count, rows)
+        for s in range(q_count):
+            q = quarter(s)
+            devs = pl.ds(q * q_devs, q_devs)
+            drain(back.at[h, devs], recv2.at[h, q])
+            x = jnp.concatenate(
+                [row_taps(f, q * q_rows, q_rows, h) for f in range(per)], axis=0
+            )
+            g = jnp.concatenate([flat(back[h, devs, f]) for f in range(per)], axis=0)
+            turned_s[...] += outer(g, x)
 
     store = pltpu.make_async_copy(feat_ref, feat_hbm, load.at[0])
     store.start()
@@ -535,7 +546,7 @@
             dma,
             dma((parts,)),
             dma,
-            dma((parts,)),
+            dma((parts, 4)),
             dma((4 + 3,)),
         ],
         compiler_params=pltpu.CompilerParams(

time: 49.9 us -> 51.3 us (1.028)
  Pallas kernels: 49.1 us -> 50.4 us
    pallas_call x1, Pallas kernels: 46.9 us -> 48.2 us  [local(): pl.pallas_call(functools.partial(kernel, n), out_shape=(jax.ShapeDtypeStr...]
where the time goes in v6:
time: 51.3 us; the launch traced here: 51.1 us
  Pallas kernels  50.4 us (98%)
  between operations  0.64 us (1%)
    pallas_call x1, Pallas kernels, local(): pl.pallas_call(functools.partial(kernel, n), out_shape=(jax.ShapeDtypeStr...  48.2 us
    pallas_call x1, Pallas kernels, widen(): pl.pallas_call(body, out_shape=(jax.ShapeDtypeStruct(features.shape, BF16...  2.21 us

profile of v6, /device:TPU:1, one launch (start us, length us, event | category | flops | bytes accessed | tf_op | source)
XLA Modules:
  0.0 51.1 jit_solution(1669472916806899813)
XLA Ops:
  0.6 48.2 %shard_map.85 = (bf16[32,64,128]{2,1,0:T(8,128)(2,1)}, bf16[2,8,80,128]{3,2,1,0:T(8,128)(2,1)}, bf16[4,4,48,128]{3,2,1,0:T(8,128)(2,1)}) custom-call(s32[2]{0:T(128)} %dil_ref.1, s32[2,3]{1,0:T(2,128)} %off_ref.1, bf16[2,32,128,128]{3,2,1,0:T(8,128)(2,1)} %frames_hbm.1, bf16[1152,128]{1,0:T(8,128)(2,1)} %bitcast.10, bf16[2,384,128]{2,1,0:T(8,128)(2,1)} %bitcast.11, ...), custom_call_target="tpu_custom_call" | custom-call | flops 2415919104 | bytes 8388608 | tf_op jit(solution)/shard_map/pallas_call | solution.py:513
  48.9 2.2 %shard_map.86 = (bf16[32,64,128]{2,1,0:T(8,128)(2,1)}, f32[1152,128]{1,0:T(8,128)}, f32[768,128]{1,0:T(8,128)}) custom-call(bf16[32,64,128]{2,1,0:T(8,128)(2,1)} %get-tuple-element.9.feat_in, bf16[1280,128]{1,0:T(8,128)(2,1)} %bitcast.6, bf16[768,128]{1,0:T(8,128)(2,1)} %bitcast.7), custom_call_target="tpu_custom_call" | custom-call | tf_op jit(solution)/shard_map/pallas_call | solution.py:479

commit v7 on v5

--- a/solution.py
+++ b/solution.py
@@ -297,15 +297,16 @@
     fetch[1].wait()
     fetch[2].wait()
 
-    def clear(t, carry):
+    def clear(i, carry):
+        h, t = i // t_count, lax.rem(i, t_count)
         zero = jnp.zeros((t_len, pp, ch), BF16)
-        s0[pl.ds(t * t_len, t_len)] = zero
-        s1[pl.ds(t * t_len, t_len)] = zero
-        d1[pl.ds(length + t * t_len, t_len)] = zero
-        d0[pl.ds(length + t * t_len, t_len)] = zero
+        s0[h, pl.ds(t * t_len, t_len)] = zero
+        s1[h, pl.ds(t * t_len, t_len)] = zero
+        d1[h, pl.ds(length + t * t_len, t_len)] = zero
+        d0[h, pl.ds(length + t * t_len, t_len)] = zero
         return carry
 
-    lax.fori_loop(0, t_count, clear, 0)
+    lax.fori_loop(0, parts * t_count, clear, 0)
     turned_s[...] = jnp.zeros_like(turned_s)
     turned_t[...] = jnp.zeros_like(turned_t)
     sum_s[sp_rows:, :] = jnp.zeros((sum_s.shape[0] - sp_rows, ch), F32)
@@ -340,33 +341,31 @@
         def forward(t):
             t0 = t * t_len
             state = land[h, pl.ds(t0, t_len)]
-            s0[pl.ds(length + t0, t_len)] = state
-            z = jnp.dot(lagged(s0, 0, t0), wt_ref[0], preferred_element_type=F32)
+            s0[h, pl.ds(length + t0, t_len)] = state
+            z = jnp.dot(lagged(s0.at[h], 0, t0), wt_ref[0], preferred_element_type=F32)
             act = unflat(jnp.tanh(z))
             act0[pl.ds(t0, t_len)] = act
             state = (state.astype(F32) + act).astype(BF16)
-            s1[pl.ds(length + t0, t_len)] = state
-            moved = lagged(s1, 1, t0)
-            act = unflat(jnp.tanh(jnp.dot(moved, wt_ref[1], preferred_element_type=F32)))
+            s1[h, pl.ds(length + t0, t_len)] = state
+            z = jnp.dot(lagged(s1.at[h], 1, t0), wt_ref[1], preferred_element_type=F32)
+            act = unflat(jnp.tanh(z))
             feat_ref[pl.ds(t0, t_len), cols] = (state.astype(F32) + act).astype(BF16)
             cot = cot_ref[pl.ds(t0, t_len), cols].astype(F32)
             dz = (cot * (1.0 - act * act)).astype(BF16)
-            d1[pl.ds(t0, t_len)] = dz
-            turned_t[1] += outer(flat(dz), moved)
+            d1[h, pl.ds(t0, t_len)] = dz
 
         steps(t_count, forward)
 
         def backward(s):
             t0 = (t_count - 1 - s) * t_len
             state = cot_ref[pl.ds(t0, t_len), cols].astype(F32) + unflat(
-                jnp.dot(led(d1, 1, t0), wback[1], preferred_element_type=F32)
+                jnp.dot(led(d1.at[h], 1, t0), wback[1], preferred_element_type=F32)
             )
             act = act0[pl.ds(t0, t_len)]
             dz = (state * (1.0 - act * act)).astype(BF16)
-            d0[pl.ds(t0, t_len)] = dz
-            state = state + unflat(jnp.dot(led(d0, 0, t0), wback[0], preferred_element_type=F32))
+            d0[h, pl.ds(t0, t_len)] = dz
+            state = state + unflat(jnp.dot(led(d0.at[h], 0, t0), wback[0], preferred_element_type=F32))
             maps[h, pl.ds(t0, t_len)] = state.astype(BF16)
-            turned_t[0] += outer(flat(dz), lagged(s0, 0, t0))
 
         steps(t_count, backward)
 
@@ -381,6 +380,14 @@
         return carry
 
     lax.fori_loop(0, parts, temporal, 0)
+
+    def temporal_grad(i, carry):
+        h, t0 = i // t_count, lax.rem(i, t_count) * t_len
+        turned_t[1] += outer(flat(d1[h, pl.ds(t0, t_len)]), lagged(s1.at[h], 1, t0))
+        turned_t[0] += outer(flat(d0[h, pl.ds(t0, t_len)]), lagged(s0.at[h], 0, t0))
+        return carry
+
+    lax.fori_loop(0, parts * t_count, temporal_grad, 0)
 
     def conv_grad(h):
         drain(back.at[h], recv2.at[h])
@@ -518,11 +525,11 @@
             pltpu.VMEM((per, out_h + 1, 2, parts, out_w // parts, 3 * ch), BF16),
             pltpu.VMEM((parts, n, per, pp, ch), BF16),
             pltpu.VMEM((parts, length, pp, ch), BF16),
-            pltpu.VMEM((2 * length, pp, ch), BF16),
-            pltpu.VMEM((2 * length, pp, ch), BF16),
+            pltpu.VMEM((parts, 2 * length, pp, ch), BF16),
+            pltpu.VMEM((parts, 2 * length, pp, ch), BF16),
             pltpu.VMEM((length, pp, ch), F32),
-            pltpu.VMEM((2 * length, pp, ch), BF16),
-            pltpu.VMEM((2 * length, pp, ch), BF16),
+            pltpu.VMEM((parts, 2 * length, pp, ch), BF16),
+            pltpu.VMEM((parts, 2 * length, pp, ch), BF16),
             pltpu.VMEM((parts, length, pp, ch), BF16),
             pltpu.VMEM((parts, n, per, pp, ch), BF16),
             pltpu.VMEM((layers, taps * ch, ch), BF16),

time: 49.9 us -> 49.2 us (0.986)
  Pallas kernels: 49.1 us -> 48.4 us
    pallas_call x1, Pallas kernels: 46.9 us -> 46.2 us  [local(): pl.pallas_call(functools.partial(kernel, n), out_shape=(jax.ShapeDtypeStr...]
where the time goes in v7:
time: 49.2 us; the launch traced here: 49.1 us
  Pallas kernels  48.4 us (98%)
  between operations  0.64 us (1%)
    pallas_call x1, Pallas kernels, local(): pl.pallas_call(functools.partial(kernel, n), out_shape=(jax.ShapeDtypeStr...  46.2 us
    pallas_call x1, Pallas kernels, widen(): pl.pallas_call(body, out_shape=(jax.ShapeDtypeStruct(features.shape, BF16...  2.21 us

profile of v7, /device:TPU:1, one launch (start us, length us, event | category | flops | bytes accessed | tf_op | source)
XLA Modules:
  0.0 49.1 jit_solution(4342563322076053673)
XLA Ops:
  0.6 46.2 %shard_map.85 = (bf16[32,64,128]{2,1,0:T(8,128)(2,1)}, bf16[2,8,80,128]{3,2,1,0:T(8,128)(2,1)}, bf16[4,4,48,128]{3,2,1,0:T(8,128)(2,1)}) custom-call(s32[2]{0:T(128)} %dil_ref.1, s32[2,3]{1,0:T(2,128)} %off_ref.1, bf16[2,32,128,128]{3,2,1,0:T(8,128)(2,1)} %frames_hbm.1, bf16[1152,128]{1,0:T(8,128)(2,1)} %bitcast.10, bf16[2,384,128]{2,1,0:T(8,128)(2,1)} %bitcast.11, ...), custom_call_target="tpu_custom_call" | custom-call | flops 2415919104 | bytes 8388608 | tf_op jit(solution)/shard_map/pallas_call | solution.py:509
  46.9 2.2 %shard_map.86 = (bf16[32,64,128]{2,1,0:T(8,128)(2,1)}, f32[1152,128]{1,0:T(8,128)}, f32[768,128]{1,0:T(8,128)}) custom-call(bf16[32,64,128]{2,1,0:T(8,128)(2,1)} %get-tuple-element.9.feat_in, bf16[1280,128]{1,0:T(8,128)(2,1)} %bitcast.6, bf16[768,128]{1,0:T(8,128)(2,1)} %bitcast.7), custom_call_target="tpu_custom_call" | custom-call | tf_op jit(solution)/shard_map/pallas_call | solution.py:475
